TPU v7x, 32 devices: a whole 2x2x4 slice. The times are simulated.
32 devices in a mesh: groups: 2 (over x), ctx: 16 (over z, y, core).
Axes of the slice: x: 2, y: 2, z: 4, core: 2. Of those that a mesh axis runs over, the one named last changes fastest.
Arguments:
- src_cache: bfloat16 [1024, 2, 2, 16, 1024], P(('groups', 'ctx')), parts along dimension 0, may hold values from -6 to 6
- src_blocks: int32 [1024], P('groups'), parts along dimension 0, may hold values from 0 to 511, as said below
- dst_blocks: int32 [1024], P('groups'), parts along dimension 0, may hold values from 0 to 511, as said below
- ctx_lengths: int32 [8], P('groups'), parts along dimension 0, may hold values from 1024 to 2048, as said below
- queries: bfloat16 [5, 2, 8, 16384], P(None, None, 'groups'), parts along dimension 2, may hold values from -120 to 120
- new_keys: bfloat16 [5, 2, 8, 1024], P(None, None, 'groups'), parts along dimension 2, may hold values from -16 to 16
- new_values: bfloat16 [5, 2, 8, 1024], P(None, None, 'groups'), parts along dimension 2, may hold values from -6 to 6
Outputs:
- dst_cache: bfloat16 [1024, 2, 2, 16, 1024], P(('groups', 'ctx')), parts along dimension 0
- attn_out: float32 [5, 2, 1024, 128], P(None, None, ('groups', 'ctx')), parts along dimension 2
There are 2 independent parts, one for each index of `groups`. A program takes and returns all parts, laid end to end along the dimension named above; each array names one. Nothing has to cross between parts.
Inputs may be any that keep to these rules, and one draw needn't show every extreme that they name: `src_blocks`: A permutation of the blocks; device k of ctx holds source slots k * 32 to (k + 1) * 32 - 1. `dst_blocks`: A permutation of the blocks; device k of ctx holds destination slots k * 32 to (k + 1) * 32 - 1. At most 2 blocks goes from the source slots of one device to the destination slots of one device, and some pair of devices has exactly 2. `ctx_lengths`: some request has exactly 2048 cached tokens.
All inputs are finite; a program needn't handle non-finite values.
Results may differ from a plain program's by a relative error of at most 0.001.
Values may be sent and summed in bfloat16 or wider, within the bound.
A program may use at most 256 MiB of HBM per device.

v0:
```python
import jax
import jax.numpy as jnp
from jax import lax
from jax.sharding import PartitionSpec as P

KVH = 8
HD = 128
QPG = 16
REQS = 4
STEPS = 4


neg_big = -1e30


def joined(value, axis, join):
    pieces = jax.tree.map(lambda part: lax.all_gather(part, axis), value)
    head = jax.tree.map(lambda part: part[0], pieces)
    tail = jax.tree.map(lambda part: part[1:], pieces)
    so_far, _ = lax.scan(lambda so_far, piece: (join(so_far, piece), None), head, tail)
    return so_far


def join_partials(earlier_part, later_part):
    max_early, total_early, sums_early = earlier_part
    max_late, total_late, sums_late = later_part
    joined_max = jnp.maximum(max_early, max_late)
    factor_early = jnp.exp(max_early - joined_max)
    factor_late = jnp.exp(max_late - joined_max)
    joined_total = total_early * factor_early + total_late * factor_late
    joined_sums = sums_early * factor_early[..., None] + sums_late * factor_late[..., None]
    return (joined_max, joined_total, joined_sums)


def migrate(src_cache, src_blocks, dst_blocks):
    devices = lax.axis_size("ctx")
    own_index = lax.axis_index("ctx")
    per_dev = src_cache.shape[0]
    block_total = src_blocks.shape[0]
    capacity = (per_dev + devices - 1) // devices
    slot_ids = jnp.arange(block_total, dtype=jnp.int32)
    inv_src = jnp.zeros((block_total,), jnp.int32).at[src_blocks].set(slot_ids)
    inv_dst = jnp.zeros((block_total,), jnp.int32).at[dst_blocks].set(slot_ids)
    target = (inv_dst[src_blocks] // per_dev).reshape(devices, per_dev)
    local_pos = jnp.arange(per_dev, dtype=jnp.int32)
    earlier = local_pos[:, None] > local_pos[None, :]
    matching = target[:, :, None] == target[:, None, :]
    bucket_rank = jnp.sum((matching & earlier[None]).astype(jnp.int32), axis=2)
    own_target = lax.dynamic_index_in_dim(target, own_index, 0, keepdims=False)
    own_rank = lax.dynamic_index_in_dim(bucket_rank, own_index, 0, keepdims=False)
    bucket = own_target * capacity + own_rank
    chosen = jnp.zeros((devices * capacity,), jnp.int32).at[bucket].set(local_pos)
    filled = jnp.zeros((devices * capacity,), jnp.int32).at[bucket].set(1) > 0
    outgoing = jnp.where(
        filled[:, None, None, None, None],
        jnp.take(src_cache, chosen, axis=0),
        jnp.zeros((), src_cache.dtype),
    )
    own_blocks = lax.dynamic_slice_in_dim(dst_blocks, own_index * per_dev, per_dev)
    root = inv_src[own_blocks]
    take_rows = root // per_dev * capacity + bucket_rank.reshape(-1)[root]
    arrived = lax.all_to_all(outgoing, "ctx", split_axis=0, concat_axis=0, tiled=True)
    return jnp.take(arrived, take_rows, axis=0)


def attend(kv_cache, block_ids, ctx_lengths, step_queries, fresh_keys, fresh_values, per_request):
    blocks, layers, _, block_len, _ = kv_cache.shape
    requests = step_queries.shape[1]
    head_rows = requests * KVH * QPG
    fresh_count = fresh_keys.shape[0]
    score_scale = HD ** (-0.5)
    highest = lax.Precision.HIGHEST
    owners = block_ids // per_request
    member = owners[:, None] == jnp.arange(requests, dtype=jnp.int32)[None, :]
    member_bf = member.astype(jnp.bfloat16)
    member_f = member.astype(jnp.float32)
    picked = jnp.einsum(
        "br,lrx->blx", member_bf, step_queries, preferred_element_type=jnp.float32
    ).astype(jnp.bfloat16)
    picked = picked.reshape(blocks, layers, KVH, QPG, HD)
    key_part = kv_cache[:, :, 0].reshape(blocks, layers, block_len, KVH, HD)
    value_part = kv_cache[:, :, 1].reshape(blocks, layers, block_len, KVH, HD)
    scores = (
        jnp.einsum("blkgd,bltkd->blkgt", picked, key_part, preferred_element_type=jnp.float32)
        * score_scale
    )
    limits = jnp.sum(jnp.where(member, ctx_lengths[None, :], 0), axis=1)
    positions = (block_ids % per_request)[:, None] * block_len + jnp.arange(
        block_len, dtype=jnp.int32
    )[None, :]
    live = (positions < limits[:, None])[:, None, None, None, :]
    scores = jnp.where(live, scores, neg_big)
    block_max = jnp.max(scores, axis=-1)
    local_max = jnp.max(
        jnp.where(member[:, :, None, None, None], block_max[:, None], neg_big), axis=0
    )
    local_max = jnp.transpose(local_max, (1, 0, 2, 3)).reshape(layers, head_rows)
    query_heads = step_queries.reshape(layers, requests, KVH, QPG, HD)
    new_key_heads = fresh_keys.reshape(fresh_count, layers, requests, KVH, HD)
    new_value_heads = fresh_values.reshape(fresh_count, layers, requests, KVH, HD).astype(
        jnp.float32
    )
    fresh_scores = (
        jnp.einsum(
            "lrkgd,slrkd->lrkgs", query_heads, new_key_heads, preferred_element_type=jnp.float32
        )
        * score_scale
    )
    fresh_max = jnp.max(fresh_scores, axis=-1).reshape(layers, head_rows)
    devices = lax.axis_size("ctx")
    share = head_rows // devices
    start = lax.axis_index("ctx") * share
    grouped = local_max.reshape(layers, requests, KVH, QPG)
    per_block = jnp.sum(jnp.where(member[:, None, :, None, None], grouped[None], 0.0), axis=2)
    weights = jnp.where(live, jnp.exp(scores - per_block[..., None]), 0.0)
    totals = jnp.einsum("br,blkg->lrkg", member_f, jnp.sum(weights, axis=-1), precision=highest)
    weighted = jnp.einsum(
        "blkgt,bltkd->blkgd", weights, value_part.astype(jnp.float32), precision=highest
    )
    weighted = jnp.einsum("br,blkgd->lrkgd", member_f, weighted, precision=highest)
    cache_totals = totals.reshape(layers, head_rows)
    cache_sums = weighted.reshape(layers, head_rows, HD)
    merged = joined((local_max, cache_totals, cache_sums), "ctx", join_partials)
    grouped = fresh_max.reshape(layers, requests, KVH, QPG)
    weights = jnp.exp(fresh_scores - grouped[..., None])
    totals = jnp.sum(weights, axis=-1).reshape(layers, head_rows)
    weighted = jnp.einsum("lrkgs,slrkd->lrkgd", weights, new_value_heads, precision=highest)
    fresh_totals = totals
    fresh_sums = weighted.reshape(layers, head_rows, HD)
    _, totals, weighted = join_partials(merged, (fresh_max, fresh_totals, fresh_sums))
    totals = lax.dynamic_slice_in_dim(totals, start, share, 1)
    weighted = lax.dynamic_slice_in_dim(weighted, start, share, 1)
    return weighted / totals[..., None]


def local(src_cache, src_blocks, dst_blocks, ctx_lengths, queries, new_keys, new_values):
    per_dev = src_cache.shape[0]
    per_request = src_blocks.shape[0] // REQS
    own_index = lax.axis_index("ctx")
    src_ids = lax.dynamic_slice_in_dim(src_blocks, own_index * per_dev, per_dev)
    dst_ids = lax.dynamic_slice_in_dim(dst_blocks, own_index * per_dev, per_dev)
    dst_cache = migrate(src_cache, src_blocks, dst_blocks)
    results = [
        attend(
            src_cache, src_ids, ctx_lengths, queries[0], new_keys[:1], new_values[:1], per_request
        )
    ]
    held_cache, held_ids = (dst_cache, dst_ids)
    for step_idx in range(1, STEPS + 1):
        results.append(
            attend(
                held_cache,
                held_ids,
                ctx_lengths,
                queries[step_idx],
                new_keys[: step_idx + 1],
                new_values[: step_idx + 1],
                per_request,
            )
        )
    return (dst_cache, jnp.stack(results))


def solution(mesh):
    in_specs = (
        P(("groups", "ctx"), None, None, None, None),
        P("groups"),
        P("groups"),
        P("groups"),
        P(None, None, "groups", None),
        P(None, None, "groups", None),
        P(None, None, "groups", None),
    )
    out_specs = (
        P(("groups", "ctx"), None, None, None, None),
        P(None, None, ("groups", "ctx"), None),
    )
    return jax.shard_map(local, mesh=mesh, in_specs=in_specs, out_specs=out_specs, check_vma=False)
```

profile of v0, /device:TPU:9, one launch (start us, length us, event | category | flops | bytes accessed | tf_op | source)
XLA Modules:
  0.0 715.5 jit_solution(13241012127152462529)
XLA Ops:
  9.3 2.7 fusion.232
  16.5 4.0 fusion.25
  25.3 1.6 copy-done.3
  26.9 5.1 fusion.30
  32.0 4.1 fusion.85
  37.0 2.4 scatter_custom_fusion
  39.5 3.5 gather_fusion
  44.3 5.1 gather_fusion.3
  50.1 4.8 select_select_fusion
  54.8 6.8 all-to-all-start
  61.7 2.4 scatter_custom_fusion.3
  66.3 2.0 copy.359
  69.9 118.0 %all-to-all-done = bf16[32,2,2,16,1024]{4,3,2,1,0:T(8,128)(2,1)} async-done(((bf16[32,2,2,16,1024]{4,3,2,1,0:T(8,128)(2,1)}), bf16[32,2,2,16,1024]{4,3,2,1,0:T(8,128)(2,1)}, u32[]{:S(2)}, u32[]{:S(2)}) %all-to-all-start) | async-done | bytes 4194336 | tf_op jit(solution)/shard_map/all_to_all | solution.py:62
  187.9 5.0 gather_fusion.4
  192.9 2.6 broadcast_select_fusion
  195.6 2.1 fusion.231
  201.5 14.4 %fusion.29 = (f32[32,2,8,16]{3,2,1,0:T(8,128)S(1)}, f32[32,2,8,16]{3,2,1,0:T(8,128)S(1)}, f32[32,2,8,16,16]{3,4,2,1,0:T(8,128)}) fusion(pred[32,16]{1,0:T(8,128)(4,1)S(1)} %add_compare_fusion, f32[32,2,8,16,16]{3,4,2,1,0:T(8,128)S(1)} %fusion.46, bf16[32,2,16,8,128]{4,3,2,1,0:T(8,128)(2,1)S(1)} %bitcast.365, bf16[32,2,8,16,128]{4,3,2,0,1:T(8,128)(2,1)S(1)} %bitcast.380), kind=kOutput, calls=%fused_computation.80 | convolution fusion | flops 34324480 | bytes 5308928 | tf_op jit(solution)/shard_map/blkgd,bltkd->blkgt/dot_general | solution.py:84
  218.5 2.4 copy.356
  221.3 5.1 fusion.32
  226.4 3.8 fusion.88
  231.9 2.0 copy.358
  234.7 1.9 copy.357
  237.5 3.6 fusion.42
  241.1 14.5 %fusion.39 = (f32[32,2,8,16]{3,2,1,0:T(8,128)}, f32[32,2,8,16]{3,2,1,0:T(8,128)}, f32[32,2,8,16]{3,2,1,0:T(8,128)}, f32[32,2,8,16]{3,2,1,0:T(8,128)}, f32[32,2,8,16,16]{3,4,2,1,0:T(8,128)}) fusion(f32[32,2,8,16,16]{3,4,2,1,0:T(8,128)} %get-tuple-element.369, f32[32,2,8,16]{3,2,1,0:T(8,128)S(1)} %copy-done.11, pred[32,16]{1,0:T(8,128)(4,1)S(1)} %add_compare_fusion, ...), kind=kOutput, calls=%fused_computation.90 | convolution fusion | flops 35618816 | bytes 6488576 | tf_op jit(solution)/shard_map/blkgd,bltkd->blkgt/dot_general | solution.py:84
  256.7 1.8 copy.300
  261.3 1.7 copy.303
  263.0 6.0 fusion.34
  269.1 3.8 fusion.91
  274.6 6.4 fusion.36
  281.1 3.8 fusion.94
  286.6 1.6 reshape.450
  290.8 2.0 reshape_squeeze.35
  294.1 4.2 fusion.31
  299.3 20.3 %all_gather.45 = f32[16,2,512]{2,1,0:T(2,128)S(1)} all-gather(f32[1,2,512]{2,1,0:T(2,128)} %all_gather_reshape.45), channel_id=1, replica_groups=mesh['groups'=2,'ctx'=16] {'ctx'}, dimensions={0}, use_global_device_ids=true | all-gather | bytes 69632 | tf_op jit(solution)/shard_map/all_gather | solution.py:17
  320.3 18.3 %all_gather.46 = f32[16,2,512]{2,1,0:T(2,128)S(1)} all-gather(f32[1,2,512]{2,1,0:T(2,128)} %all_gather_reshape.46), channel_id=1, replica_groups=mesh['groups'=2,'ctx'=16] {'ctx'}, dimensions={0}, use_global_device_ids=true | all-gather | bytes 69632 | tf_op jit(solution)/shard_map/all_gather | solution.py:17
  349.2 1.9 fusion.235
  362.4 1.8 broadcast_multiply_fusion
  364.2 2.3 fusion.126
  366.5 2.4 fusion.116
  368.8 2.3 fusion.118
  373.7 19.0 %all_gather.48 = f32[16,2,512]{2,1,0:T(2,128)S(1)} all-gather(f32[1,2,512]{2,1,0:T(2,128)S(1)} %all_gather_reshape.48), channel_id=1, replica_groups=mesh['groups'=2,'ctx'=16] {'ctx'}, dimensions={0}, use_global_device_ids=true | all-gather | bytes 69632 | tf_op jit(solution)/shard_map/all_gather | solution.py:17
  392.7 17.9 %all_gather.49 = f32[16,2,512]{2,1,0:T(2,128)S(1)} all-gather(f32[1,2,512]{2,1,0:T(2,128)S(1)} %all_gather_reshape.49), channel_id=1, replica_groups=mesh['groups'=2,'ctx'=16] {'ctx'}, dimensions={0}, use_global_device_ids=true | all-gather | bytes 69632 | tf_op jit(solution)/shard_map/all_gather | solution.py:17
  411.5 5.9 fusion.37
  417.8 19.4 %all_gather.51 = f32[16,2,512]{2,1,0:T(2,128)S(1)} all-gather(f32[1,2,512]{2,1,0:T(2,128)S(1)} %all_gather_reshape.51), channel_id=1, replica_groups=mesh['groups'=2,'ctx'=16] {'ctx'}, dimensions={0}, use_global_device_ids=true | all-gather | bytes 69632 | tf_op jit(solution)/shard_map/all_gather | solution.py:17
  437.2 18.1 %all_gather.52 = f32[16,2,512]{2,1,0:T(2,128)S(1)} all-gather(f32[1,2,512]{2,1,0:T(2,128)S(1)} %all_gather_reshape.52), channel_id=1, replica_groups=mesh['groups'=2,'ctx'=16] {'ctx'}, dimensions={0}, use_global_device_ids=true | all-gather | bytes 69632 | tf_op jit(solution)/shard_map/all_gather | solution.py:17
  455.8 18.9 %all_gather.54 = f32[16,2,512]{2,1,0:T(2,128)S(1)} all-gather(f32[1,2,512]{2,1,0:T(2,128)S(1)} %all_gather_reshape.54), channel_id=1, replica_groups=mesh['groups'=2,'ctx'=16] {'ctx'}, dimensions={0}, use_global_device_ids=true | all-gather | bytes 69632 | tf_op jit(solution)/shard_map/all_gather | solution.py:17
  474.7 17.9 %all_gather.55 = f32[16,2,512]{2,1,0:T(2,128)S(1)} all-gather(f32[1,2,512]{2,1,0:T(2,128)S(1)} %all_gather_reshape.55), channel_id=1, replica_groups=mesh['groups'=2,'ctx'=16] {'ctx'}, dimensions={0}, use_global_device_ids=true | all-gather | bytes 69632 | tf_op jit(solution)/shard_map/all_gather | solution.py:17
  493.1 6.0 fusion.38
  499.1 3.8 fusion.97
  503.8 18.8 %all_gather.57 = f32[16,2,512]{2,1,0:T(2,128)S(1)} all-gather(f32[1,2,512]{2,1,0:T(2,128)S(1)} %all_gather_reshape.57), channel_id=1, replica_groups=mesh['groups'=2,'ctx'=16] {'ctx'}, dimensions={0}, use_global_device_ids=true | all-gather | bytes 69632 | tf_op jit(solution)/shard_map/all_gather | solution.py:17
  522.6 18.0 %all_gather.58 = f32[16,2,512]{2,1,0:T(2,128)S(1)} all-gather(f32[1,2,512]{2,1,0:T(2,128)S(1)} %all_gather_reshape.58), channel_id=1, replica_groups=mesh['groups'=2,'ctx'=16] {'ctx'}, dimensions={0}, use_global_device_ids=true | all-gather | bytes 69632 | tf_op jit(solution)/shard_map/all_gather | solution.py:17
  541.8 7.1 slice.209
  549.0 23.4 %while.70 = (s32[]{:T(128)}, f32[2,512]{1,0:T(2,128)S(1)}, f32[2,512]{1,0:T(2,128)S(1)}, f32[2,512,128]{2,1,0:T(8,128)S(1)}, f32[15,2,512]{2,1,0:T(2,128)S(1)}, ...) while((s32[]{:T(128)}, f32[2,512]{1,0:T(2,128)S(1)}, f32[2,512]{1,0:T(2,128)S(1)}, ...), condition=%wide.region_11.13_spmd, body=%wide.region_10.12_spmd.sunk | while | flops 399362 | bytes 1613925 | solution.py:20
  550.6 1.6 fusion.266
  575.2 8.0 %slice.217 = f32[15,2,512,128]{3,2,1,0:T(8,128)} slice(f32[16,2,512,128]{3,2,1,0:T(8,128)} %all-gather.8.cloned.1.call-done), slice={[1:16], [0:2], [0:512], [0:128]} | slice | bytes 15728640 | tf_op jit(solution)/shard_map/slice | solution.py:19
  583.2 23.5 %while.71 = (s32[]{:T(128)}, f32[2,512]{1,0:T(2,128)S(1)}, f32[2,512]{1,0:T(2,128)S(1)}, f32[2,512,128]{2,1,0:T(8,128)S(1)}, f32[15,2,512]{2,1,0:T(2,128)S(1)}, ...) while((s32[]{:T(128)}, f32[2,512]{1,0:T(2,128)S(1)}, f32[2,512]{1,0:T(2,128)S(1)}, ...), condition=%wide.region_18.20_spmd, body=%wide.region_17.19_spmd.sunk | while | flops 399362 | bytes 1613925 | solution.py:20
  583.2 1.6 fusion.268
  600.4 1.7 fusion.268
  606.7 7.2 %slice.223 = f32[15,2,512,128]{3,2,1,0:T(8,128)} slice(f32[16,2,512,128]{3,2,1,0:T(8,128)} %all-gather.10.cloned.1.call-done), slice={[1:16], [0:2], [0:512], [0:128]} | slice | bytes 15728640 | tf_op jit(solution)/shard_map/slice | solution.py:19
  613.9 7.2 %slice.229 = f32[15,2,512,128]{3,2,1,0:T(8,128)} slice(f32[16,2,512,128]{3,2,1,0:T(8,128)} %all-gather.12.cloned.1.call-done), slice={[1:16], [0:2], [0:512], [0:128]} | slice | bytes 15728640 | tf_op jit(solution)/shard_map/slice | solution.py:19
  623.3 23.3 %while.72 = (s32[]{:T(128)}, f32[2,512]{1,0:T(2,128)S(1)}, f32[2,512]{1,0:T(2,128)S(1)}, f32[2,512,128]{2,1,0:T(8,128)S(1)}, f32[15,2,512]{2,1,0:T(2,128)S(1)}, ...) while((s32[]{:T(128)}, f32[2,512]{1,0:T(2,128)S(1)}, f32[2,512]{1,0:T(2,128)S(1)}, ...), condition=%wide.region_26.28_spmd, body=%wide.region_25.27_spmd.sunk | while | flops 399362 | bytes 1613925 | solution.py:20
  646.6 23.3 %while.73 = (s32[]{:T(128)}, f32[2,512]{1,0:T(2,128)S(1)}, f32[2,512]{1,0:T(2,128)S(1)}, f32[2,512,128]{2,1,0:T(8,128)S(1)}, f32[15,2,512]{2,1,0:T(2,128)S(1)}, ...) while((s32[]{:T(128)}, f32[2,512]{1,0:T(2,128)S(1)}, f32[2,512]{1,0:T(2,128)S(1)}, ...), condition=%wide.region_34.36_spmd, body=%wide.region_33.35_spmd.sunk | while | flops 399362 | bytes 1613925 | solution.py:20
  671.1 7.2 %slice.235 = f32[15,2,512,128]{3,2,1,0:T(8,128)} slice(f32[16,2,512,128]{3,2,1,0:T(8,128)} %all-gather.14.cloned.1.call-done), slice={[1:16], [0:2], [0:512], [0:128]} | slice | bytes 15728640 | tf_op jit(solution)/shard_map/slice | solution.py:19
  678.3 23.3 %while.74 = (s32[]{:T(128)}, f32[2,512]{1,0:T(2,128)S(1)}, f32[2,512]{1,0:T(2,128)S(1)}, f32[2,512,128]{2,1,0:T(8,128)S(1)}, f32[15,2,512]{2,1,0:T(2,128)S(1)}, ...) while((s32[]{:T(128)}, f32[2,512]{1,0:T(2,128)S(1)}, f32[2,512]{1,0:T(2,128)S(1)}, ...), condition=%wide.region_42.44_spmd, body=%wide.region_41.43_spmd.sunk | while | flops 399362 | bytes 1613925 | solution.py:20
  (490 shorter events, 193.2 us)
Async XLA Ops:
  7.2 533.5 %all-gather.6.cloned.1.call-start = ((), (), s32[]{:S(2)}) async-start(), calls=%async_computation.1 | async-start | bytes 8912896 | tf_op jit(solution)/shard_map/all_gather | solution.py:17
  14.0 18.0 %copy-start.60 = (s32[32]{0:T(128)}, s32[32]{0:T(128)S(1)}, u32[]{:S(2)}) copy-start(s32[32]{0:T(128)S(1)} %get-tuple-element.379) | copy-start | bytes 388
  14.0 267.1 %copy-start.51 = (s32[32]{0:T(128)}, s32[32]{0:T(128)S(1)}, u32[]{:S(2)}) copy-start(s32[32]{0:T(128)S(1)} %get-tuple-element.363) | copy-start | bytes 388
  16.5 8.8 %copy-start.53 = (pred[32,16]{1,0:T(8,128)(4,1)}, pred[32,16]{1,0:T(8,128)(4,1)S(1)}, u32[]{:S(2)}) copy-start(pred[32,16]{1,0:T(8,128)(4,1)S(1)} %add_compare_fusion.1) | copy-start | bytes 1540
  54.8 133.0 %all-to-all-start = ((bf16[32,2,2,16,1024]{4,3,2,1,0:T(8,128)(2,1)}), bf16[32,2,2,16,1024]{4,3,2,1,0:T(8,128)(2,1)}, u32[]{:S(2)}, u32[]{:S(2)}) async-start(bf16[32,2,2,16,1024]{4,3,2,1,0:T(8,128)(2,1)} %select_select_fusion), calls=%async_computation | async-start | bytes 8388608 | tf_op jit(solution)/shard_map/all_to_all | solution.py:62
  61.6 512.5 %all-gather.8.cloned.1.call-start = ((), (), s32[]{:S(2)}) async-start(), calls=%async_computation.2 | async-start | bytes 8912896 | tf_op jit(solution)/shard_map/all_gather | solution.py:17
  69.8 146.4 %copy-start.62 = (pred[32,4]{0,1:T(4,128)(4,1)}, pred[32,4]{0,1:T(4,128)(4,1)S(1)}, u32[]{:S(2)}) copy-start(pred[32,4]{0,1:T(4,128)(4,1)S(1)} %iota_compare_fusion.1) | copy-start | bytes 388
  69.9 204.8 %copy-start.49 = (pred[32,16]{1,0:T(8,128)(4,1)}, pred[32,16]{1,0:T(8,128)(4,1)S(1)}, u32[]{:S(2)}) copy-start(pred[32,16]{1,0:T(8,128)(4,1)S(1)} %add_compare_fusion) | copy-start | bytes 1540
  200.1 15.8 %copy-start.4 = (f32[32,2,8,16,16]{3,4,2,1,0:T(8,128)}, f32[32,2,8,16,16]{3,4,2,1,0:T(8,128)S(1)}, u32[]{:S(2)}) copy-start(f32[32,2,8,16,16]{3,4,2,1,0:T(8,128)S(1)} %fusion.46) | copy-start | bytes 1572868
  231.1 375.6 %all-gather.10.cloned.1.call-start = ((), (), s32[]{:S(2)}) async-start(), calls=%async_computation.3 | async-start | bytes 8912896 | tf_op jit(solution)/shard_map/all_gather | solution.py:17
  241.0 14.5 %copy-start = (f32[32,2,8,16,16]{3,4,2,1,0:T(8,128)}, f32[32,2,8,16,16]{3,4,2,1,0:T(8,128)S(1)}, u32[]{:S(2)}) copy-start(f32[32,2,8,16,16]{3,4,2,1,0:T(8,128)S(1)} %fusion.42) | copy-start | bytes 1572868
  241.1 17.4 %copy-start.63 = (pred[32,4]{0,1:T(4,128)(4,1)S(1)}, pred[32,4]{0,1:T(4,128)(4,1)}, u32[]{:S(2)}) copy-start(pred[32,4]{0,1:T(4,128)(4,1)} %copy-done.62) | copy-start | bytes 388
  273.8 340.2 %all-gather.12.cloned.1.call-start = ((), (), s32[]{:S(2)}) async-start(), calls=%async_computation.4 | async-start | bytes 8912896 | tf_op jit(solution)/shard_map/all_gather | solution.py:17
  281.1 11.7 %slice-start = ((bf16[5,2,4,1024]{3,2,1,0:T(4,128)(2,1)}), bf16[1,2,4,1024]{3,2,1,0:T(4,128)(2,1)S(1)}, s32[]{:S(2)}) async-start(bf16[5,2,4,1024]{3,2,1,0:T(4,128)(2,1)} %param.24), calls=%async_computation.6 | async-start | bytes 32768 | tf_op jit(solution)/shard_map/slice | solution.py:145
  281.1 12.3 %copy-start.24 = (f32[4,2,8,16]{3,2,1,0:T(8,128)S(1)}, f32[4,2,8,16]{3,2,1,0:T(8,128)}, u32[]{:S(2)}) copy-start(f32[4,2,8,16]{3,2,1,0:T(8,128)} %copy-done.23) | copy-start | bytes 12292
  281.1 13.0 %copy-start.54 = (pred[32,16]{1,0:T(8,128)(4,1)S(1)}, pred[32,16]{1,0:T(8,128)(4,1)}, u32[]{:S(2)}) copy-start(pred[32,16]{1,0:T(8,128)(4,1)} %copy-done.53) | copy-start | bytes 1540
  285.8 384.1 %all-gather.14.cloned.1.call-start = ((), (), s32[]{:S(2)}) async-start(), calls=%async_computation.5 | async-start | bytes 8912896 | tf_op jit(solution)/shard_map/all_gather | solution.py:17
  285.9 12.5 %copy-start.61 = (s32[32]{0:T(128)S(1)}, s32[32]{0:T(128)}, u32[]{:S(2)}) copy-start(s32[32]{0:T(128)} %copy-done.60) | copy-start | bytes 388
  290.8 52.4 %copy-start.16 = (bf16[1,2,4,16384]{3,2,1,0:T(4,128)(2,1)S(1)}, bf16[1,2,4,16384]{3,2,1,0:T(4,128)(2,1)}, u32[]{:S(2)}) copy-start(bf16[1,2,4,16384]{3,2,1,0:T(4,128)(2,1)} %get-tuple-element.348) | copy-start | bytes 786436
  290.8 53.3 %slice-start.1 = ((bf16[5,2,4,1024]{3,2,1,0:T(4,128)(2,1)}), bf16[2,2,4,1024]{3,2,1,0:T(4,128)(2,1)S(1)}, s32[]{:S(2)}) async-start(bf16[5,2,4,1024]{3,2,1,0:T(4,128)(2,1)} %param.24), calls=%async_computation.7 | async-start | bytes 65536 | tf_op jit(solution)/shard_map/slice | solution.py:156
  290.8 53.4 %slice-start.4 = ((bf16[5,2,4,1024]{3,2,1,0:T(4,128)(2,1)}), bf16[2,2,4,1024]{3,2,1,0:T(4,128)(2,1)S(1)}, s32[]{:S(2)}) async-start(bf16[5,2,4,1024]{3,2,1,0:T(4,128)(2,1)} %param.25), calls=%async_computation.10 | async-start | bytes 65536 | tf_op jit(solution)/shard_map/slice | solution.py:157
  290.8 56.7 %copy-start.15 = (bf16[1,2,4,16384]{3,2,1,0:T(4,128)(2,1)S(1)}, bf16[1,2,4,16384]{3,2,1,0:T(4,128)(2,1)}, u32[]{:S(2)}) copy-start(bf16[1,2,4,16384]{3,2,1,0:T(4,128)(2,1)} %get-tuple-element.347) | copy-start | bytes 786436
  290.8 57.7 %slice-start.2 = ((bf16[5,2,4,1024]{3,2,1,0:T(4,128)(2,1)}), bf16[3,2,4,1024]{3,2,1,0:T(4,128)(2,1)S(1)}, s32[]{:S(2)}) async-start(bf16[5,2,4,1024]{3,2,1,0:T(4,128)(2,1)} %param.24), calls=%async_computation.8 | async-start | bytes 98304 | tf_op jit(solution)/shard_map/slice | solution.py:156
  292.8 55.7 %slice-start.5 = ((bf16[5,2,4,1024]{3,2,1,0:T(4,128)(2,1)}), bf16[3,2,4,1024]{3,2,1,0:T(4,128)(2,1)S(1)}, s32[]{:S(2)}) async-start(bf16[5,2,4,1024]{3,2,1,0:T(4,128)(2,1)} %param.25), calls=%async_computation.11 | async-start | bytes 98304 | tf_op jit(solution)/shard_map/slice | solution.py:157
  294.1 59.3 %copy-start.14 = (bf16[1,2,4,16384]{3,2,1,0:T(4,128)(2,1)S(1)}, bf16[1,2,4,16384]{3,2,1,0:T(4,128)(2,1)}, u32[]{:S(2)}) copy-start(bf16[1,2,4,16384]{3,2,1,0:T(4,128)(2,1)} %get-tuple-element.350) | copy-start | bytes 786436
  294.1 60.3 %slice-start.3 = ((bf16[5,2,4,1024]{3,2,1,0:T(4,128)(2,1)}), bf16[4,2,4,1024]{3,2,1,0:T(4,128)(2,1)S(1)}, s32[]{:S(2)}) async-start(bf16[5,2,4,1024]{3,2,1,0:T(4,128)(2,1)} %param.24), calls=%async_computation.9 | async-start | bytes 131072 | tf_op jit(solution)/shard_map/slice | solution.py:156
  294.1 60.4 %slice-start.6 = ((bf16[5,2,4,1024]{3,2,1,0:T(4,128)(2,1)}), bf16[4,2,4,1024]{3,2,1,0:T(4,128)(2,1)S(1)}, s32[]{:S(2)}) async-start(bf16[5,2,4,1024]{3,2,1,0:T(4,128)(2,1)} %param.25), calls=%async_computation.12 | async-start | bytes 131072 | tf_op jit(solution)/shard_map/slice | solution.py:157
  294.1 63.7 %copy-start.13 = (bf16[1,2,4,16384]{3,2,1,0:T(4,128)(2,1)S(1)}, bf16[1,2,4,16384]{3,2,1,0:T(4,128)(2,1)}, u32[]{:S(2)}) copy-start(bf16[1,2,4,16384]{3,2,1,0:T(4,128)(2,1)} %get-tuple-element.346) | copy-start | bytes 786436
  298.4 59.8 %copy-start.19 = (bf16[5,2,4,8,128]{4,3,2,1,0:T(8,128)(2,1)S(1)}, bf16[5,2,4,8,128]{4,3,2,1,0:T(8,128)(2,1)}, u32[]{:S(2)}) copy-start(bf16[5,2,4,8,128]{4,3,2,1,0:T(8,128)(2,1)} %reshape.448) | copy-start | bytes 245764
  347.5 25.1 %copy-start.26 = (f32[4,2,8,16]{3,2,1,0:T(8,128)S(1)}, f32[4,2,8,16]{3,2,1,0:T(8,128)}, u32[]{:S(2)}) copy-start(f32[4,2,8,16]{3,2,1,0:T(8,128)} %copy-done.25) | copy-start | bytes 12292
  348.5 22.6 %copy-start.20 = (bf16[5,2,4,8,128]{4,3,2,1,0:T(8,128)(2,1)S(1)}, bf16[5,2,4,8,128]{4,3,2,1,0:T(8,128)(2,1)}, u32[]{:S(2)}) copy-start(bf16[5,2,4,8,128]{4,3,2,1,0:T(8,128)(2,1)} %reshape.450) | copy-start | bytes 245764
  351.1 60.4 %copy-start.8 = (f32[32,2,8,16]{3,2,1,0:T(8,128)S(1)}, f32[32,2,8,16]{3,2,1,0:T(8,128)}, u32[]{:S(2)}) copy-start(f32[32,2,8,16]{3,2,1,0:T(8,128)} %copy.303) | copy-start | bytes 98308
  351.1 60.4 %copy-start.9 = (f32[32,2,8,16]{3,2,1,0:T(8,128)S(1)}, f32[32,2,8,16]{3,2,1,0:T(8,128)}, u32[]{:S(2)}) copy-start(f32[32,2,8,16]{3,2,1,0:T(8,128)} %copy.317) | copy-start | bytes 98308
  358.4 14.3 %copy-start.35 = (f32[32,2,8,16]{3,2,1,0:T(8,128)S(1)}, f32[32,2,8,16]{3,2,1,0:T(8,128)}, u32[]{:S(2)}) copy-start(f32[32,2,8,16]{3,2,1,0:T(8,128)} %get-tuple-element.214) | copy-start | bytes 98308
  392.7 147.9 %copy-start.38 = (f32[16,2,512]{2,1,0:T(2,128)}, f32[16,2,512]{2,1,0:T(2,128)S(1)}, u32[]{:S(2)}) copy-start(f32[16,2,512]{2,1,0:T(2,128)S(1)} %all_gather.48) | copy-start | bytes 196612
  411.5 43.8 %copy-start.28 = (f32[4,2,8,16]{3,2,1,0:T(8,128)S(1)}, f32[4,2,8,16]{3,2,1,0:T(8,128)}, u32[]{:S(2)}) copy-start(f32[4,2,8,16]{3,2,1,0:T(8,128)} %copy-done.27) | copy-start | bytes 12292
  411.5 81.1 %copy-start.22 = (f32[4,2,8,16]{3,2,1,0:T(8,128)S(1)}, f32[4,2,8,16]{3,2,1,0:T(8,128)}, u32[]{:S(2)}) copy-start(f32[4,2,8,16]{3,2,1,0:T(8,128)} %copy-done.21) | copy-start | bytes 12292
  411.5 81.2 %copy-start.34 = (f32[32,2,8,16]{3,2,1,0:T(8,128)S(1)}, f32[32,2,8,16]{3,2,1,0:T(8,128)}, u32[]{:S(2)}) copy-start(f32[32,2,8,16]{3,2,1,0:T(8,128)} %get-tuple-element.213) | copy-start | bytes 98308
  411.5 81.6 %copy-start.12 = (f32[32,2,8,16]{3,2,1,0:T(8,128)S(1)}, f32[32,2,8,16]{3,2,1,0:T(8,128)}, u32[]{:S(2)}) copy-start(f32[32,2,8,16]{3,2,1,0:T(8,128)} %copy.331) | copy-start | bytes 98308
  411.5 81.6 %copy-start.50 = (pred[32,16]{1,0:T(8,128)(4,1)S(1)}, pred[32,16]{1,0:T(8,128)(4,1)}, u32[]{:S(2)}) copy-start(pred[32,16]{1,0:T(8,128)(4,1)} %copy-done.49) | copy-start | bytes 1540
  437.2 103.4 %copy-start.41 = (f32[16,2,512]{2,1,0:T(2,128)}, f32[16,2,512]{2,1,0:T(2,128)S(1)}, u32[]{:S(2)}) copy-start(f32[16,2,512]{2,1,0:T(2,128)S(1)} %all_gather.51) | copy-start | bytes 196612
  455.3 85.3 %copy-start.42 = (f32[16,2,512]{2,1,0:T(2,128)}, f32[16,2,512]{2,1,0:T(2,128)S(1)}, u32[]{:S(2)}) copy-start(f32[16,2,512]{2,1,0:T(2,128)S(1)} %all_gather.52) | copy-start | bytes 196612
  474.7 65.9 %copy-start.43 = (f32[16,2,512]{2,1,0:T(2,128)}, f32[16,2,512]{2,1,0:T(2,128)S(1)}, u32[]{:S(2)}) copy-start(f32[16,2,512]{2,1,0:T(2,128)S(1)} %all_gather.54) | copy-start | bytes 196612
  492.6 48.0 %copy-start.44 = (f32[16,2,512]{2,1,0:T(2,128)}, f32[16,2,512]{2,1,0:T(2,128)S(1)}, u32[]{:S(2)}) copy-start(f32[16,2,512]{2,1,0:T(2,128)S(1)} %all_gather.55) | copy-start | bytes 196612
  499.1 41.4 %copy-start.40 = (f32[16,2,512]{2,1,0:T(2,128)S(1)}, f32[16,2,512]{2,1,0:T(2,128)}, u32[]{:S(2)}) copy-start(f32[16,2,512]{2,1,0:T(2,128)} %copy-done.39) | copy-start | bytes 196612
  522.6 26.4 %copy-start.45 = (f32[16,2,512]{2,1,0:T(2,128)}, f32[16,2,512]{2,1,0:T(2,128)S(1)}, u32[]{:S(2)}) copy-start(f32[16,2,512]{2,1,0:T(2,128)S(1)} %all_gather.57) | copy-start | bytes 196612
  540.5 8.4 %copy-start.46 = (f32[16,2,512]{2,1,0:T(2,128)}, f32[16,2,512]{2,1,0:T(2,128)S(1)}, u32[]{:S(2)}) copy-start(f32[16,2,512]{2,1,0:T(2,128)S(1)} %all_gather.58) | copy-start | bytes 196612
  541.8 7.2 %slice-start.7 = ((f32[16,2,512]{2,1,0:T(2,128)}), f32[15,2,512]{2,1,0:T(2,128)S(1)}, s32[]{:S(2)}) async-start(f32[16,2,512]{2,1,0:T(2,128)} %copy-done.36), calls=%async_computation.13 | async-start | bytes 122880 | tf_op jit(solution)/shard_map/slice | solution.py:19
  541.8 7.2 %slice-start.8 = ((f32[16,2,512]{2,1,0:T(2,128)}), f32[15,2,512]{2,1,0:T(2,128)S(1)}, s32[]{:S(2)}) async-start(f32[16,2,512]{2,1,0:T(2,128)} %copy-done.37), calls=%async_computation.14 | async-start | bytes 122880 | tf_op jit(solution)/shard_map/slice | solution.py:19
  541.8 7.2 %copy-start.47 = (f32[2,512]{1,0:T(2,128)S(1)}, f32[2,512]{1,0:T(2,128)}, u32[]{:S(2)}) copy-start(f32[2,512]{1,0:T(2,128)} %slice_bitcast_fusion.14) | copy-start | bytes 12292
  541.8 7.2 %copy-start.48 = (f32[2,512]{1,0:T(2,128)S(1)}, f32[2,512]{1,0:T(2,128)}, u32[]{:S(2)}) copy-start(f32[2,512]{1,0:T(2,128)} %slice_bitcast_fusion.13) | copy-start | bytes 12292
  549.0 23.5 %copy-start.59 = (f32[2,512]{1,0:T(2,128)S(1)}, f32[2,512]{1,0:T(2,128)}, u32[]{:S(2)}) copy-start(f32[2,512]{1,0:T(2,128)} %reshape.425) | copy-start | bytes 12292
  575.2 8.0 %slice-start.9 = ((f32[16,2,512]{2,1,0:T(2,128)}), f32[15,2,512]{2,1,0:T(2,128)S(1)}, s32[]{:S(2)}) async-start(f32[16,2,512]{2,1,0:T(2,128)} %copy-done.38), calls=%async_computation.15 | async-start | bytes 122880 | tf_op jit(solution)/shard_map/slice | solution.py:19
  575.2 8.0 %slice-start.10 = ((f32[16,2,512]{2,1,0:T(2,128)}), f32[15,2,512]{2,1,0:T(2,128)S(1)}, s32[]{:S(2)}) async-start(f32[16,2,512]{2,1,0:T(2,128)} %copy-done.39), calls=%async_computation.16 | async-start | bytes 122880 | tf_op jit(solution)/shard_map/slice | solution.py:19
  613.9 9.3 %slice-start.11 = ((f32[16,2,512]{2,1,0:T(2,128)}), f32[15,2,512]{2,1,0:T(2,128)S(1)}, s32[]{:S(2)}) async-start(f32[16,2,512]{2,1,0:T(2,128)} %copy-done.41), calls=%async_computation.17 | async-start | bytes 122880 | tf_op jit(solution)/shard_map/slice | solution.py:19
  613.9 9.3 %slice-start.12 = ((f32[16,2,512]{2,1,0:T(2,128)}), f32[15,2,512]{2,1,0:T(2,128)S(1)}, s32[]{:S(2)}) async-start(f32[16,2,512]{2,1,0:T(2,128)} %copy-done.42), calls=%async_computation.18 | async-start | bytes 122880 | tf_op jit(solution)/shard_map/slice | solution.py:19
  623.3 23.3 %slice-start.13 = ((f32[16,2,512]{2,1,0:T(2,128)}), f32[15,2,512]{2,1,0:T(2,128)S(1)}, s32[]{:S(2)}) async-start(f32[16,2,512]{2,1,0:T(2,128)} %copy-done.43), calls=%async_computation.19 | async-start | bytes 122880 | tf_op jit(solution)/shard_map/slice | solution.py:19
  623.3 23.3 %slice-start.14 = ((f32[16,2,512]{2,1,0:T(2,128)}), f32[15,2,512]{2,1,0:T(2,128)S(1)}, s32[]{:S(2)}) async-start(f32[16,2,512]{2,1,0:T(2,128)} %copy-done.44), calls=%async_computation.20 | async-start | bytes 122880 | tf_op jit(solution)/shard_map/slice | solution.py:19
  671.0 7.2 %slice-start.15 = ((f32[16,2,512]{2,1,0:T(2,128)}), f32[15,2,512]{2,1,0:T(2,128)S(1)}, s32[]{:S(2)}) async-start(f32[16,2,512]{2,1,0:T(2,128)} %copy-done.45), calls=%async_computation.21 | async-start | bytes 122880 | tf_op jit(solution)/shard_map/slice | solution.py:19
  671.0 7.2 %slice-start.16 = ((f32[16,2,512]{2,1,0:T(2,128)}), f32[15,2,512]{2,1,0:T(2,128)S(1)}, s32[]{:S(2)}) async-start(f32[16,2,512]{2,1,0:T(2,128)} %copy-done.46), calls=%async_computation.22 | async-start | bytes 122880 | tf_op jit(solution)/shard_map/slice | solution.py:19
  678.2 23.3 %copy-start.55 = (f32[2,512]{1,0:T(2,128)S(1)}, f32[2,512]{1,0:T(2,128)}, u32[]{:S(2)}) copy-start(f32[2,512]{1,0:T(2,128)} %reshape.431) | copy-start | bytes 12292
  678.2 23.4 %copy-start.56 = (f32[2,512]{1,0:T(2,128)S(1)}, f32[2,512]{1,0:T(2,128)}, u32[]{:S(2)}) copy-start(f32[2,512]{1,0:T(2,128)} %reshape.437) | copy-start | bytes 12292
  678.3 23.4 %copy-start.57 = (f32[2,512]{1,0:T(2,128)S(1)}, f32[2,512]{1,0:T(2,128)}, u32[]{:S(2)}) copy-start(f32[2,512]{1,0:T(2,128)} %reshape.443) | copy-start | bytes 12292
  678.3 23.4 %copy-start.58 = (f32[2,512]{1,0:T(2,128)S(1)}, f32[2,512]{1,0:T(2,128)}, u32[]{:S(2)}) copy-start(f32[2,512]{1,0:T(2,128)} %reshape.449) | copy-start | bytes 12292
  (30 other events, 80.8 us)
Sparse Core Ops, SparseCore 0:
  37.1 134.3 all-gather.5
  231.2 76.5 all-gather.7
  310.0 73.5 all-gather.9
  385.6 74.4 all-gather.11
  540.8 75.2 all-gather.13
where the time goes:
time: 728 us; the launch traced here: 716 us
  blocking collectives  187 us (26%)
  other arithmetic  156 us (21%)
  local copies, waits for them, and re-layouts  125 us (17%)
  waiting for transfers between devices  118 us (16%)
  matrix products  106 us (15%)
  between operations  15.5 us (2%)
    all_gather x10, blocking collectives, joined(): pieces = jax.tree.map(lambda part: lax.all_gather(part, axis), value)  187 us
    all_to_all x1, waiting for transfers between devices, migrate(): lax.all_to_all(outgoing, 'ctx', split_axis=0, concat_axis=0, tiled=True)  118 us
    add x75, other arithmetic, join_partials(): sums_early * factor_early[..., None] + sums_late * factor_late[..., None]  113 us
    dot_general x5, matrix products, attend(): jnp.einsum('blkgd,bltkd->blkgt', picked, key_part, preferred_element_type...  37.7 us
    slice x25, local copies, waits for them, and re-layouts, joined(): tail = jax.tree.map(lambda part: part[1:], pieces)  36.7 us
    dot_general x5, matrix products, attend(): jnp.einsum('blkgt,bltkd->blkgd', weights, value_part.astype(jnp.float32),...  28.6 us
    dot_general x5, matrix products, attend(): jnp.einsum('br,blkgd->lrkgd', member_f, weighted, precision=highest)  19.3 us
    unnamed x151, local copies, waits for them, and re-layouts  18.6 us
  transfers between devices with their start and end apart: 6, of which 1 were waited for; matrix products, arithmetic and copies ran while one was open for 44% of the time, Pallas kernels for 0%

commit v1 on v0

v1 whole, which is shorter than its diff:
```python
import functools

import jax
import jax.numpy as jnp
from jax import lax
from jax.experimental import pallas as pl
from jax.experimental.pallas import tpu as pltpu
from jax.sharding import PartitionSpec as P

KVH = 8
HD = 128
QPG = 16
REQS = 4

NEG_BIG = -1e30
STAT_ROWS = 8
MESH = pl.DeviceIdType.MESH


def move_blocks(index_ref, src_ref, out_ref, sems):
    count = out_ref.shape[0]

    def copy(i):
        return pltpu.make_async_copy(src_ref.at[index_ref[i]], out_ref.at[i], sems.at[i])

    lax.fori_loop(0, count, lambda i, c: (copy(i).start(), c)[1], 0)
    lax.fori_loop(0, count, lambda i, c: (copy(i).wait(), c)[1], 0)


def take_blocks(src, index):
    count = index.shape[0]
    return pl.pallas_call(
        move_blocks,
        out_shape=jax.ShapeDtypeStruct((count,) + src.shape[1:], src.dtype),
        in_specs=[
            pl.BlockSpec(memory_space=pltpu.SMEM),
            pl.BlockSpec(memory_space=pl.ANY),
        ],
        out_specs=pl.BlockSpec(memory_space=pl.ANY),
        scratch_shapes=[pltpu.SemaphoreType.DMA((count,))],
        name="take_blocks",
    )(index, src)


def split_bf16(value):
    high = value.astype(jnp.bfloat16)
    low = (value - high.astype(jnp.float32)).astype(jnp.bfloat16)
    return high, low


def dot(a, b, b_dim):
    return lax.dot_general(
        a, b, (((1,), (b_dim,)), ((), ())), preferred_element_type=jnp.float32
    )


def exchange_kernel(
    n,
    groups,
    halves,
    out_blocks,
    cache,
    queries,
    fresh_keys,
    fresh_values,
    token_request,
    fresh_bias,
    arrived,
    result,
    acc,
    acc_in,
    stat,
    stat_in,
    stat_cols,
    block_send,
    block_recv,
    acc_send,
    acc_recv,
    stat_send,
    stat_recv,
    own_sems,
):
    me = lax.axis_index("ctx")
    blocks, layers, _, block_len, _ = cache.shape
    tokens = blocks * block_len
    rows = acc.shape[3]
    width = rows * halves

    def peer(k):
        return lax.rem(me + k, n)

    def each(body):
        lax.fori_loop(1, n, lambda k, c: (body(k), c)[1], 0)

    barrier = pltpu.get_barrier_semaphore()
    each(lambda k: pl.semaphore_signal(barrier, 1, device_id={"ctx": peer(k)}, device_id_type=MESH))
    pl.semaphore_wait(barrier, n - 1)

    def remote(src, dst, send, recv, k):
        return pltpu.make_async_remote_copy(
            src_ref=src.at[peer(k)],
            dst_ref=dst.at[me],
            send_sem=send.at[k],
            recv_sem=recv.at[k],
            device_id={"ctx": peer(k)},
            device_id_type=MESH,
        )

    def block_copy(k):
        return remote(out_blocks, arrived, block_send, block_recv, k)

    def acc_copy(k):
        return remote(acc, acc_in, acc_send, acc_recv, k)

    def stat_copy(k):
        return remote(stat, stat_in, stat_send, stat_recv, k)

    each(lambda k: block_copy(k).start())
    own_blocks = pltpu.make_async_copy(out_blocks.at[me], arrived.at[me], own_sems.at[0])
    own_blocks.start()

    stat_cols[...] = jnp.zeros_like(stat_cols)
    lane = lax.broadcasted_iota(jnp.int32, (1, HD), 1)
    fresh_live = jnp.where(me == 0, 0.0, NEG_BIG)

    def head(g, carry):
        cols = pl.ds(pl.multiple_of(g * HD, HD), HD)
        for layer in range(layers):
            q = queries[layer, g]
            k_cache = cache[:, layer, 0, :, cols].reshape(tokens, HD)
            v_cache = cache[:, layer, 1, :, cols].reshape(tokens, HD)
            k_new = fresh_keys[layer, :, cols]
            v_new = fresh_values[layer, :, cols]
            scores = dot(q, k_cache, 1) * (HD**-0.5)
            new_scores = dot(q, k_new, 1) * (HD**-0.5)
            for r in range(REQS):
                part = slice(r * width, (r + 1) * width)
                live = jnp.where(token_request[...] == r, 0.0, NEG_BIG)
                s = scores[part] + live
                s_new = new_scores[part] + (fresh_bias[part] + fresh_live)
                top = jnp.maximum(
                    jnp.max(s, axis=1, keepdims=True), jnp.max(s_new, axis=1, keepdims=True)
                )
                w = jnp.exp(s - top)
                w_new = jnp.exp(s_new - top)
                total = jnp.sum(w, axis=1, keepdims=True) + jnp.sum(w_new, axis=1, keepdims=True)
                high, low = split_bf16(w)
                new_high, new_low = split_bf16(w_new)
                sums = (
                    dot(high, v_cache, 0)
                    + dot(low, v_cache, 0)
                    + dot(new_high, v_new, 0)
                    + dot(new_low, v_new, 0)
                )
                for h in range(halves):
                    chunk = (r * KVH + g) * halves + h
                    acc[chunk // groups, chunk % groups, layer] = sums[h * rows : (h + 1) * rows]
                at = g * STAT_ROWS + layer
                now = stat_cols[part]
                now = jnp.where(lane == at, top, now)
                stat_cols[part] = jnp.where(lane == at + layers, total, now)
        return carry

    lax.fori_loop(0, KVH, head, 0)

    pad = jnp.zeros((HD - rows, HD), jnp.float32)
    for r in range(REQS):
        for h in range(halves):
            start = (r * halves + h) * rows
            turned = jnp.concatenate([stat_cols[start : start + rows], pad], axis=0).T
            for g in range(KVH):
                chunk = (r * KVH + g) * halves + h
                stat[chunk // groups, chunk % groups] = turned[
                    g * STAT_ROWS : (g + 1) * STAT_ROWS
                ]

    each(lambda k: (stat_copy(k).start(), acc_copy(k).start()))
    own_acc = pltpu.make_async_copy(acc.at[me], acc_in.at[me], own_sems.at[1])
    own_stat = pltpu.make_async_copy(stat.at[me], stat_in.at[me], own_sems.at[2])
    own_acc.start()
    own_stat.start()
    own_acc.wait()
    own_stat.wait()
    each(lambda k: (stat_copy(k).wait(), acc_copy(k).wait()))

    share = rows // result.shape[0]
    for gi in range(groups):
        for layer in range(layers):
            tops = stat_in[:, gi, layer, :]
            top = jnp.max(tops, axis=0, keepdims=True)
            factor = jnp.exp(tops - top)
            total = jnp.sum(factor * stat_in[:, gi, layers + layer, :], axis=0, keepdims=True)
            factor = factor / total
            factor = jnp.concatenate([factor, jnp.zeros((HD - n, HD), jnp.float32)], axis=0).T
            out = jnp.zeros((rows, HD), jnp.float32)
            for src in range(n):
                out = out + factor[:rows, src : src + 1] * acc_in[src, gi, layer]
            for step in range(result.shape[0]):
                result[step, layer, gi * share : (gi + 1) * share, :] = out[
                    step * share : (step + 1) * share
                ]

    own_blocks.wait()
    each(lambda k: block_copy(k).wait())


def exchange(n, outgoing, cache, queries, fresh_keys, fresh_values, token_request):
    steps, layers, requests, _ = queries.shape
    share = requests * KVH * QPG // n
    groups = max(share // QPG, 1)
    halves = max(QPG // share, 1)
    heads = QPG // halves
    rows = steps * heads
    q = queries.reshape(steps, layers, requests, KVH, halves, heads, HD)
    q = jnp.transpose(q, (1, 3, 2, 4, 0, 5, 6)).reshape(
        layers, KVH, requests * halves * rows, HD
    )
    fresh = steps * requests
    fresh_pad = -(-fresh // 16) * 16

    def fresh_rows(value):
        value = jnp.transpose(value, (1, 0, 2, 3)).reshape(layers, fresh, KVH * HD)
        return jnp.pad(value, ((0, 0), (0, fresh_pad - fresh), (0, 0)))

    row = jnp.arange(requests * halves * rows)
    row_request = row // (halves * rows)
    row_step = row % rows // heads
    col = jnp.arange(fresh_pad)
    seen = (
        (col[None, :] % requests == row_request[:, None])
        & (col[None, :] // requests <= row_step[:, None])
        & (col[None, :] < fresh)
    )
    fresh_bias = jnp.where(seen, 0.0, NEG_BIG).astype(jnp.float32)
    vmem = pl.BlockSpec(memory_space=pltpu.VMEM)
    hbm = pl.BlockSpec(memory_space=pl.ANY)
    dma = pltpu.SemaphoreType.DMA
    return pl.pallas_call(
        functools.partial(exchange_kernel, n, groups, halves),
        out_shape=(
            jax.ShapeDtypeStruct(outgoing.shape, outgoing.dtype),
            jax.ShapeDtypeStruct((steps, layers, share, HD), jnp.float32),
        ),
        in_specs=[hbm] + [vmem] * 6,
        out_specs=(hbm, vmem),
        scratch_shapes=[
            pltpu.VMEM((n, groups, layers, rows, HD), jnp.float32),
            pltpu.VMEM((n, groups, layers, rows, HD), jnp.float32),
            pltpu.VMEM((n, groups, STAT_ROWS, HD), jnp.float32),
            pltpu.VMEM((n, groups, STAT_ROWS, HD), jnp.float32),
            pltpu.VMEM((requests * halves * rows, HD), jnp.float32),
            dma((n,)),
            dma((n,)),
            dma((n,)),
            dma((n,)),
            dma((n,)),
            dma((n,)),
            dma((3,)),
        ],
        compiler_params=pltpu.CompilerParams(
            collective_id=0, has_side_effects=True, vmem_limit_bytes=48 * 1024 * 1024
        ),
        name="exchange",
    )(outgoing, cache, q, fresh_rows(fresh_keys), fresh_rows(fresh_values), token_request, fresh_bias)


def local(src_cache, src_blocks, dst_blocks, ctx_lengths, queries, new_keys, new_values):
    n = lax.axis_size("ctx")
    me = lax.axis_index("ctx")
    per_dev, _, _, block_len, _ = src_cache.shape
    total = src_blocks.shape[0]
    per_request = total // REQS
    cap = (per_dev + n - 1) // n
    slots = jnp.arange(total, dtype=jnp.int32)
    pos = jnp.arange(per_dev, dtype=jnp.int32)
    src_ids = lax.dynamic_slice_in_dim(src_blocks, me * per_dev, per_dev)
    dst_ids = lax.dynamic_slice_in_dim(dst_blocks, me * per_dev, per_dev)

    target = jnp.sum(jnp.where(src_ids[:, None] == dst_blocks[None], slots[None], 0), axis=1) // per_dev
    before = (target[:, None] == target[None]) & (pos[None] < pos[:, None])
    bucket = target * cap + jnp.sum(before.astype(jnp.int32), axis=1)
    bucket_ids = jnp.arange(n * cap, dtype=jnp.int32)
    chosen = jnp.sum(jnp.where(bucket_ids[:, None] == bucket[None], pos[None], 0), axis=1)

    root = jnp.sum(jnp.where(dst_ids[:, None] == src_blocks[None], slots[None], 0), axis=1)
    owner = root // per_dev
    earlier = (owner[:, None] == owner[None]) & (root[None] < root[:, None])
    rows = owner * cap + jnp.sum(earlier.astype(jnp.int32), axis=1)

    request = src_ids // per_request
    limit = jnp.sum(
        jnp.where(request[:, None] == jnp.arange(REQS)[None], ctx_lengths[None], 0), axis=1
    )
    at = (src_ids % per_request)[:, None] * block_len + jnp.arange(block_len)[None]
    token_request = jnp.where(at < limit[:, None], request[:, None], -1).astype(jnp.int32)
    token_request = token_request.reshape(1, per_dev * block_len)

    outgoing = take_blocks(src_cache, chosen)
    outgoing = outgoing.reshape((n, cap) + src_cache.shape[1:])
    arrived, attn = exchange(
        n, outgoing, src_cache, queries, new_keys, new_values, token_request
    )
    dst_cache = take_blocks(arrived.reshape((n * cap,) + src_cache.shape[1:]), rows)
    return dst_cache, attn


def solution(mesh):
    in_specs = (
        P(("groups", "ctx"), None, None, None, None),
        P("groups"),
        P("groups"),
        P("groups"),
        P(None, None, "groups", None),
        P(None, None, "groups", None),
        P(None, None, "groups", None),
    )
    out_specs = (
        P(("groups", "ctx"), None, None, None, None),
        P(None, None, ("groups", "ctx"), None),
    )
    return jax.shard_map(local, mesh=mesh, in_specs=in_specs, out_specs=out_specs, check_vma=False)
```

time: 728 us -> 432 us (0.59); the launches traced: 716 us -> 430 us
  Pallas kernels: 0 us -> 416 us
  blocking collectives: 187 us -> 0 us
  other arithmetic: 156 us -> 5.13 us
  waiting for transfers between devices: 118 us -> 0 us
  local copies, waits for them, and re-layouts: 125 us -> 8.75 us
  matrix products: 106 us -> 0 us
  between operations: 15.5 us -> 0.75 us
    pallas_call x0 -> x3, Pallas kernels: none -> 416 us  [the longest x2 258 us: take_blocks(): pl.pallas_call(move_blocks, out_shape=jax.ShapeDtypeStruct((count,) + src...]
    all_gather x10 -> x0, blocking collectives: 187 us -> none  [joined(): pieces = jax.tree.map(lambda part: lax.all_gather(part, axis), value)]
    add x155 -> x2, other arithmetic: 119 us -> 0.55 us  [the longest x1 0.53 us: local(): rows = owner * cap + jnp.sum(earlier.astype(jnp.int32), axis=1)]
    all_to_all x1 -> x0, waiting for transfers between devices: 118 us -> none  [migrate(): lax.all_to_all(outgoing, 'ctx', split_axis=0, concat_axis=0, tiled=True)]
    dot_general x34 -> x0, matrix products: 106 us -> none  [the longest x5 37.7 us: attend(): jnp.einsum('blkgd,bltkd->blkgt', picked, key_part, preferred_element_type...]
    slice x42 -> x0, local copies, waits for them, and re-layouts: 42.8 us -> none  [the longest x25 36.7 us: joined(): tail = jax.tree.map(lambda part: part[1:], pieces)]
    unnamed x151 -> x3, local copies, waits for them, and re-layouts: 18.6 us -> 2.59 us
    gather x6 -> x0, local copies, waits for them, and re-layouts: 15.1 us -> none  [the longest x1 5.13 us: migrate(): jnp.take(src_cache, chosen, axis=0)]
  transfers between devices with their start and end apart: 6 -> 0, of which waited for: 1 -> 0; matrix products, arithmetic and copies ran while one was open for 44% -> 0% of each run, Pallas kernels for 0% -> 0%
where the time goes in v1:
time: 432 us; the launch traced here: 430 us
  Pallas kernels  416 us (96%)
  local copies, waits for them, and re-layouts  8.75 us (2%)
  other arithmetic  5.13 us (1%)
    pallas_call x2, Pallas kernels, take_blocks(): pl.pallas_call(move_blocks, out_shape=jax.ShapeDtypeStruct((count,) + src...  258 us
    pallas_call x1, Pallas kernels, exchange(): pl.pallas_call(functools.partial(exchange_kernel, n, groups, halves), out...  157 us

profile of v1, /device:TPU:9, one launch (start us, length us, event | category | flops | bytes accessed | tf_op | source)
XLA Modules:
  0.0 430.2 jit_solution(10718548756248460173)
XLA Ops:
  0.6 0.8 dynamic_slice.6
  1.4 0.9 select_reduce_fusion.1
  2.3 0.2 convert_reduce_fusion.1
  2.5 0.5 multiply_add_fusion.1.index_ref
  3.0 0.8 fusion.11
  3.8 0.9 select_reduce_fusion
  4.6 0.2 convert_reduce_fusion
  4.8 0.7 select_reduce_fusion.2.index_ref
  5.6 0.7 select_reduce_fusion.3
  6.3 0.1 fusion.1
  6.4 0.1 select_n.131.token_request
  6.5 1.0 copy.18
  7.5 1.0 copy.20
  8.5 0.2 and_select_fusion.fresh_bias
  8.6 3.0 reshape.249
  11.7 0.3 copy.17
  12.0 129.1 %take_blocks.2 = bf16[32,2,2,16,1024]{4,3,2,1,0:T(8,128)(2,1)} custom-call(s32[32]{0:T(128)} %select_reduce_fusion.2.index_ref, bf16[32,2,2,16,1024]{4,3,2,1,0:T(8,128)(2,1)} %cache.1), custom_call_target="tpu_custom_call" | custom-call | tf_op jit(solution)/shard_map/take_blocks/pallas_call | solution.py:32
  141.1 157.3 %exchange.1 = (bf16[16,2,2,2,16,1024]{5,4,3,2,1,0:T(8,128)(2,1)S(1)}, f32[5,2,32,128]{3,2,1,0:T(8,128)S(1)}) custom-call(bf16[16,2,2,2,16,1024]{5,4,3,2,1,0:T(8,128)(2,1)} %bitcast.11, bf16[32,2,2,16,1024]{4,3,2,1,0:T(8,128)(2,1)} %cache.1, bf16[2,8,320,128]{3,2,1,0:T(8,128)(2,1)S(1)} %bitcast.9, bf16[2,32,1024]{2,1,0:T(8,128)(2,1)S(1)} %pad.7.fresh_keys, ...), custom_call_target="tpu_custom_call" | custom-call | tf_op jit(solution)/shard_map/exchange/pallas_call | solution.py:238
  298.5 0.0 copy-start
  298.5 1.9 copy-done
  300.4 129.1 %take_blocks.3 = bf16[32,2,2,16,1024]{4,3,2,1,0:T(8,128)(2,1)} custom-call(s32[32]{0:T(128)} %multiply_add_fusion.1.index_ref, bf16[32,2,2,16,1024]{4,3,2,1,0:T(8,128)(2,1)} %bitcast.10), custom_call_target="tpu_custom_call" | custom-call | tf_op jit(solution)/shard_map/take_blocks/pallas_call | solution.py:32
  429.5 0.7 copy.23
  (11 shorter events, 0.1 us)
Async XLA Ops:
  298.5 1.9 copy-start

commit v2 on v1

v2 whole, which is shorter than its diff:
```python
import functools

import jax
import jax.numpy as jnp
from jax import lax
from jax.experimental import pallas as pl
from jax.experimental.pallas import tpu as pltpu
from jax.sharding import PartitionSpec as P

KVH = 8
HD = 128
QPG = 16
REQS = 4

NEG_BIG = -1e30
STAT_ROWS = 8
MESH = pl.DeviceIdType.MESH


def split_bf16(value):
    high = value.astype(jnp.bfloat16)
    low = (value - high.astype(jnp.float32)).astype(jnp.bfloat16)
    return high, low


def dot(a, b, b_dim):
    return lax.dot_general(
        a, b, (((1,), (b_dim,)), ((), ())), preferred_element_type=jnp.float32
    )


def exchange_kernel(
    n,
    groups,
    halves,
    send_index,
    take_index,
    cache,
    queries,
    fresh_keys,
    fresh_values,
    token_request,
    fresh_bias,
    placed,
    result,
    outgoing,
    arrived,
    acc,
    acc_core,
    acc_near,
    acc_far,
    stat,
    stat_core,
    stat_near,
    stat_far,
    stat_cols,
    block_send,
    block_recv,
    pair_send,
    pair_recv,
    far_send,
    far_recv,
):
    me = lax.axis_index("ctx")
    blocks, layers, _, block_len, _ = cache.shape
    tokens = blocks * block_len
    cap = outgoing.shape[1]
    quarter = n // 4
    rows = acc.shape[5]
    width = rows * halves
    bit0 = lax.rem(me, 2)
    bit1 = lax.rem(me // 2, 2)
    high = me // 4

    def loop(start, stop, body):
        lax.fori_loop(start, stop, lambda k, c: (body(k), c)[1], 0)

    def peer(k):
        return lax.rem(me + k, n)

    def send(src, dst, send_sem, recv_sem, device):
        return pltpu.make_async_remote_copy(
            src_ref=src,
            dst_ref=dst,
            send_sem=send_sem,
            recv_sem=recv_sem,
            device_id={"ctx": device},
            device_id_type=MESH,
        )

    barrier = pltpu.get_barrier_semaphore()
    loop(
        1,
        n,
        lambda k: pl.semaphore_signal(
            barrier, 1, device_id={"ctx": peer(k)}, device_id_type=MESH
        ),
    )
    pl.semaphore_wait(barrier, n - 1)

    def block_copy(k):
        return send(
            outgoing.at[peer(k)], arrived.at[me], block_send.at[k], block_recv.at[k], peer(k)
        )

    def send_blocks(k):
        for c in range(cap):
            outgoing[peer(k), c] = cache[send_index[peer(k) * cap + c]]
        block_copy(k).start()

    loop(1, n, send_blocks)
    for c in range(cap):
        arrived[me, c] = cache[send_index[me * cap + c]]

    stat_cols[...] = jnp.zeros_like(stat_cols)
    lane = lax.broadcasted_iota(jnp.int32, (1, HD), 1)
    fresh_live = jnp.where(me == 0, 0.0, NEG_BIG)

    def head(g):
        cols = pl.ds(pl.multiple_of(g * HD, HD), HD)
        for layer in range(layers):
            q = queries[layer, g]
            k_cache = cache[:, layer, 0, :, cols].reshape(tokens, HD)
            v_cache = cache[:, layer, 1, :, cols].reshape(tokens, HD)
            k_new = fresh_keys[layer, :, cols]
            v_new = fresh_values[layer, :, cols]
            scores = dot(q, k_cache, 1) * (HD**-0.5)
            new_scores = dot(q, k_new, 1) * (HD**-0.5)
            for r in range(REQS):
                part = slice(r * width, (r + 1) * width)
                live = jnp.where(token_request[...] == r, 0.0, NEG_BIG)
                s = scores[part] + live
                s_new = new_scores[part] + (fresh_bias[part] + fresh_live)
                top = jnp.maximum(
                    jnp.max(s, axis=1, keepdims=True), jnp.max(s_new, axis=1, keepdims=True)
                )
                w = jnp.exp(s - top)
                w_new = jnp.exp(s_new - top)
                total = jnp.sum(w, axis=1, keepdims=True) + jnp.sum(w_new, axis=1, keepdims=True)
                big, small = split_bf16(w)
                new_big, new_small = split_bf16(w_new)
                sums = (
                    dot(big, v_cache, 0)
                    + dot(small, v_cache, 0)
                    + dot(new_big, v_new, 0)
                    + dot(new_small, v_new, 0)
                )
                for h in range(halves):
                    chunk = (r * KVH + g) * halves + h
                    to, gi = chunk // groups, chunk % groups
                    acc[to % 2, to // 2 % 2, to // 4, gi, layer] = sums[h * rows : (h + 1) * rows]
                at = g * STAT_ROWS + layer
                now = stat_cols[part]
                now = jnp.where(lane == at, top, now)
                stat_cols[part] = jnp.where(lane == at + layers, total, now)

    loop(0, KVH, head)

    pad = jnp.zeros((HD - rows, HD), jnp.float32)
    for r in range(REQS):
        for h in range(halves):
            start = (r * halves + h) * rows
            turned = jnp.concatenate([stat_cols[start : start + rows], pad], axis=0).T
            for g in range(KVH):
                chunk = (r * KVH + g) * halves + h
                to, gi = chunk // groups, chunk % groups
                stat[to % 2, to // 2 % 2, to // 4, gi] = turned[
                    g * STAT_ROWS : (g + 1) * STAT_ROWS
                ]

    def columns(factors):
        filler = jnp.zeros((HD - factors.shape[0], HD), jnp.float32)
        return jnp.concatenate([factors, filler], axis=0).T

    def join(acc_own, stat_own, acc_new, stat_new):
        for gi in range(groups):
            a, b = stat_own[gi], stat_new[gi]
            top = jnp.maximum(a[:layers], b[:layers])
            keep = jnp.exp(a[:layers] - top)
            add = jnp.exp(b[:layers] - top)
            total = a[layers : 2 * layers] * keep + b[layers : 2 * layers] * add
            filler = jnp.zeros((STAT_ROWS - 2 * layers, HD), jnp.float32)
            stat_own[gi] = jnp.concatenate([top, total, filler], axis=0)
            factor = columns(jnp.concatenate([keep, add], axis=0))
            for layer in range(layers):
                acc_own[gi, layer] = (
                    acc_own[gi, layer] * factor[:rows, layer : layer + 1]
                    + acc_new[gi, layer] * factor[:rows, layers + layer : layers + layer + 1]
                )

    def swap(copies):
        for copy in copies:
            copy.start()
        for copy in copies:
            copy.wait()

    core = me + 1 - 2 * bit0
    swap(
        [
            send(stat.at[1 - bit0], stat_core, pair_send.at[0], pair_recv.at[0], core),
            send(acc.at[1 - bit0], acc_core, pair_send.at[1], pair_recv.at[1], core),
        ]
    )

    def join_core(i):
        b, z = i // quarter, lax.rem(i, quarter)
        join(
            acc.at[bit0, b, z], stat.at[bit0, b, z], acc_core.at[b, z], stat_core.at[b, z]
        )

    loop(0, 2 * quarter, join_core)

    near = me + 2 - 4 * bit1
    swap(
        [
            send(stat.at[bit0, 1 - bit1], stat_near, pair_send.at[2], pair_recv.at[2], near),
            send(acc.at[bit0, 1 - bit1], acc_near, pair_send.at[3], pair_recv.at[3], near),
        ]
    )
    loop(
        0,
        quarter,
        lambda z: join(
            acc.at[bit0, bit1, z], stat.at[bit0, bit1, z], acc_near.at[z], stat_near.at[z]
        ),
    )

    def far_copies(k):
        to = lax.rem(high + k, quarter)
        device = to * 4 + lax.rem(me, 4)
        return (
            send(
                stat.at[bit0, bit1, to],
                stat_far.at[high],
                far_send.at[0, k],
                far_recv.at[0, k],
                device,
            ),
            send(
                acc.at[bit0, bit1, to], acc_far.at[high], far_send.at[1, k], far_recv.at[1, k], device
            ),
        )

    loop(1, quarter, lambda k: [copy.start() for copy in far_copies(k)])
    stat_far[high] = stat[bit0, bit1, high]
    acc_far[high] = acc[bit0, bit1, high]
    loop(1, quarter, lambda k: [copy.wait() for copy in far_copies(k)])

    share = rows // result.shape[0]
    for gi in range(groups):
        for layer in range(layers):
            tops = stat_far[:, gi, layer, :]
            top = jnp.max(tops, axis=0, keepdims=True)
            factor = jnp.exp(tops - top)
            total = jnp.sum(factor * stat_far[:, gi, layers + layer, :], axis=0, keepdims=True)
            factor = columns(factor / total)
            out = jnp.zeros((rows, HD), jnp.float32)
            for src in range(quarter):
                out = out + factor[:rows, src : src + 1] * acc_far[src, gi, layer]
            for step in range(result.shape[0]):
                result[step, layer, gi * share : (gi + 1) * share, :] = out[
                    step * share : (step + 1) * share
                ]

    loop(1, n, lambda k: block_copy(k).wait())

    def place(j):
        at = take_index[j]
        placed[j] = arrived[at // cap, lax.rem(at, cap)]

    loop(0, blocks, place)


def exchange(n, cap, send_index, take_index, cache, queries, fresh_keys, fresh_values, token_request):
    steps, layers, requests, _ = queries.shape
    share = requests * KVH * QPG // n
    groups = max(share // QPG, 1)
    halves = max(QPG // share, 1)
    heads = QPG // halves
    rows = steps * heads
    q = queries.reshape(steps, layers, requests, KVH, halves, heads, HD)
    q = jnp.transpose(q, (1, 3, 2, 4, 0, 5, 6)).reshape(
        layers, KVH, requests * halves * rows, HD
    )
    fresh = steps * requests
    fresh_pad = -(-fresh // 16) * 16

    def fresh_rows(value):
        value = jnp.transpose(value, (1, 0, 2, 3)).reshape(layers, fresh, KVH * HD)
        return jnp.pad(value, ((0, 0), (0, fresh_pad - fresh), (0, 0)))

    row = jnp.arange(requests * halves * rows)
    row_request = row // (halves * rows)
    row_step = row % rows // heads
    col = jnp.arange(fresh_pad)
    seen = (
        (col[None, :] % requests == row_request[:, None])
        & (col[None, :] // requests <= row_step[:, None])
        & (col[None, :] < fresh)
    )
    fresh_bias = jnp.where(seen, 0.0, NEG_BIG).astype(jnp.float32)
    quarter = n // 4
    block = cache.shape[1:]
    piece = (groups, layers, rows, HD)
    note = (groups, STAT_ROWS, HD)
    vmem = pl.BlockSpec(memory_space=pltpu.VMEM)
    smem = pl.BlockSpec(memory_space=pltpu.SMEM)
    dma = pltpu.SemaphoreType.DMA
    f32 = jnp.float32
    return pl.pallas_call(
        functools.partial(exchange_kernel, n, groups, halves),
        out_shape=(
            jax.ShapeDtypeStruct(cache.shape, cache.dtype),
            jax.ShapeDtypeStruct((steps, layers, share, HD), f32),
        ),
        in_specs=[smem] * 2 + [vmem] * 6,
        out_specs=(vmem, vmem),
        scratch_shapes=[
            pltpu.VMEM((n, cap) + block, cache.dtype),
            pltpu.VMEM((n, cap) + block, cache.dtype),
            pltpu.VMEM((2, 2, quarter) + piece, f32),
            pltpu.VMEM((2, quarter) + piece, f32),
            pltpu.VMEM((quarter,) + piece, f32),
            pltpu.VMEM((quarter,) + piece, f32),
            pltpu.VMEM((2, 2, quarter) + note, f32),
            pltpu.VMEM((2, quarter) + note, f32),
            pltpu.VMEM((quarter,) + note, f32),
            pltpu.VMEM((quarter,) + note, f32),
            pltpu.VMEM((requests * halves * rows, HD), f32),
            dma((n,)),
            dma((n,)),
            dma((4,)),
            dma((4,)),
            dma((2, quarter)),
            dma((2, quarter)),
        ],
        compiler_params=pltpu.CompilerParams(
            collective_id=0, has_side_effects=True, vmem_limit_bytes=56 * 1024 * 1024
        ),
        name="exchange",
    )(
        send_index,
        take_index,
        cache,
        q,
        fresh_rows(fresh_keys),
        fresh_rows(fresh_values),
        token_request,
        fresh_bias,
    )


def local(src_cache, src_blocks, dst_blocks, ctx_lengths, queries, new_keys, new_values):
    n = lax.axis_size("ctx")
    me = lax.axis_index("ctx")
    per_dev, _, _, block_len, _ = src_cache.shape
    total = src_blocks.shape[0]
    per_request = total // REQS
    cap = (per_dev + n - 1) // n
    slots = jnp.arange(total, dtype=jnp.int32)
    pos = jnp.arange(per_dev, dtype=jnp.int32)
    src_ids = lax.dynamic_slice_in_dim(src_blocks, me * per_dev, per_dev)
    dst_ids = lax.dynamic_slice_in_dim(dst_blocks, me * per_dev, per_dev)

    target = jnp.sum(jnp.where(src_ids[:, None] == dst_blocks[None], slots[None], 0), axis=1) // per_dev
    before = (target[:, None] == target[None]) & (pos[None] < pos[:, None])
    bucket = target * cap + jnp.sum(before.astype(jnp.int32), axis=1)
    bucket_ids = jnp.arange(n * cap, dtype=jnp.int32)
    chosen = jnp.sum(jnp.where(bucket_ids[:, None] == bucket[None], pos[None], 0), axis=1)

    root = jnp.sum(jnp.where(dst_ids[:, None] == src_blocks[None], slots[None], 0), axis=1)
    owner = root // per_dev
    earlier = (owner[:, None] == owner[None]) & (root[None] < root[:, None])
    rows = owner * cap + jnp.sum(earlier.astype(jnp.int32), axis=1)

    request = src_ids // per_request
    limit = jnp.sum(
        jnp.where(request[:, None] == jnp.arange(REQS)[None], ctx_lengths[None], 0), axis=1
    )
    at = (src_ids % per_request)[:, None] * block_len + jnp.arange(block_len)[None]
    token_request = jnp.where(at < limit[:, None], request[:, None], -1).astype(jnp.int32)
    token_request = token_request.reshape(1, per_dev * block_len)

    return exchange(
        n, cap, chosen, rows, src_cache, queries, new_keys, new_values, token_request
    )


def solution(mesh):
    in_specs = (
        P(("groups", "ctx"), None, None, None, None),
        P("groups"),
        P("groups"),
        P("groups"),
        P(None, None, "groups", None),
        P(None, None, "groups", None),
        P(None, None, "groups", None),
    )
    out_specs = (
        P(("groups", "ctx"), None, None, None, None),
        P(None, None, ("groups", "ctx"), None),
    )
    return jax.shard_map(local, mesh=mesh, in_specs=in_specs, out_specs=out_specs, check_vma=False)
```

time: 432 us -> 139 us (0.32)
  Pallas kernels: 416 us -> 117 us
  local copies, waits for them, and re-layouts: 8.75 us -> 14.9 us
    pallas_call x2 -> x0, Pallas kernels: 258 us -> none  [take_blocks(): pl.pallas_call(move_blocks, out_shape=jax.ShapeDtypeStruct((count,) + src...]
    pallas_call x1, Pallas kernels: 157 us -> 117 us  [exchange(): pl.pallas_call(functools.partial(exchange_kernel, n, groups, halves), out...]
where the time goes in v2:
time: 139 us; the launch traced here: 138 us
  Pallas kernels  117 us (84%)
  local copies, waits for them, and re-layouts  14.9 us (11%)
  other arithmetic  5.84 us (4%)
    pallas_call x1, Pallas kernels, exchange(): pl.pallas_call(functools.partial(exchange_kernel, n, groups, halves), out...  117 us
    unnamed x4, local copies, waits for them, and re-layouts  5.75 us
    reshape x2, local copies, waits for them, and re-layouts, exchange(): q = queries.reshape(steps, layers, requests, KVH, halves, heads, HD)  4.44 us

profile of v2, /device:TPU:9, one launch (start us, length us, event | category | flops | bytes accessed | tf_op | source)
XLA Modules:
  0.0 138.2 jit_solution(17159076379627917957)
XLA Ops:
  0.6 0.8 dynamic_slice.7
  1.4 0.9 select_reduce_fusion
  2.3 0.2 convert_reduce_fusion
  2.5 0.6 multiply_add_fusion.take_index
  3.1 0.8 fusion.11
  3.8 0.9 select_reduce_fusion.1
  4.7 0.2 convert_reduce_fusion.1
  4.9 0.7 select_reduce_fusion.2.send_index
  5.6 0.7 select_reduce_fusion.3
  6.4 0.1 fusion.1
  6.4 0.7 select_n.131.token_request
  7.1 0.9 copy.18
  8.1 0.7 pad.7.fresh_keys
  8.7 0.9 copy.20
  9.7 0.7 pad.8.fresh_values
  10.4 0.8 and_select_fusion.fresh_bias
  11.2 3.0 %reshape.242 = bf16[5,2,4,8,1,16,128]{6,5,3,2,1,0,4:T(8,128)(2,1)S(1)} reshape(bf16[5,2,4,16384]{3,2,1,0:T(4,128)(2,1)} %param.11) | data formatting | bytes 2621440 | tf_op jit(solution)/shard_map/reshape | solution.py:281
  14.2 1.4 %copy.17 = bf16[5,2,4,8,1,16,128]{6,5,0,2,3,1,4:T(8,128)(2,1)} copy(bf16[5,2,4,8,1,16,128]{6,5,3,2,1,0,4:T(8,128)(2,1)S(1)} %reshape.242) | data formatting | bytes 2621440 | tf_op jit(solution)/shard_map/reshape | solution.py:281
  15.6 116.8 %exchange.1 = (bf16[32,2,2,16,1024]{4,3,2,1,0:T(8,128)(2,1)}, f32[5,2,32,128]{3,2,1,0:T(8,128)}) custom-call(s32[32]{0:T(128)} %select_reduce_fusion.2.send_index, s32[32]{0:T(128)} %multiply_add_fusion.take_index, bf16[32,2,2,16,1024]{4,3,2,1,0:T(8,128)(2,1)} %cache.1, bf16[2,8,320,128]{3,2,1,0:T(8,128)(2,1)} %bitcast.7, ...), custom_call_target="tpu_custom_call" | custom-call | tf_op jit(solution)/shard_map/exchange/pallas_call | solution.py:310
  132.4 0.0 copy-start
  132.4 5.1 %copy.24 = bf16[32,2,2,16,1024]{4,3,2,1,0:T(8,128)(2,1)} copy(bf16[32,2,2,16,1024]{4,3,2,1,0:T(8,128)(2,1)} %get-tuple-element.10) | data formatting | bytes 8388608
  137.5 0.0 copy-done
  137.5 0.7 copy.25
  (9 shorter events, 0.1 us)
Async XLA Ops:
  132.4 5.1 %copy-start = (f32[5,2,32,128]{3,2,1,0:T(8,128)S(1)}, f32[5,2,32,128]{3,2,1,0:T(8,128)}, u32[]{:S(2)}) copy-start(f32[5,2,32,128]{3,2,1,0:T(8,128)} %get-tuple-element.11) | copy-start | bytes 491524

commit v3 on v2

--- a/solution.py
+++ b/solution.py
@@ -17,6 +17,109 @@
 MESH = pl.DeviceIdType.MESH
 
 
+def plan_kernel(
+    n, per_dev, block_len, per_request, src_ref, dst_ref, lengths, send_index, take_index, tokens_of
+):
+    me = lax.axis_index("ctx")
+    cap = (per_dev + n - 1) // n
+    total = src_ref.shape[1]
+    f32 = jnp.float32
+
+    def iota(cols, axis):
+        return lax.broadcasted_iota(jnp.int32, (per_dev, cols), axis).astype(f32)
+
+    def over(row, by):
+        return jnp.floor(row * (1.0 / by))
+
+    src, dst = src_ref[...].astype(f32), dst_ref[...].astype(f32)
+    lane, sub = iota(total, 1), iota(total, 0)
+    own = lane == sub + (me * per_dev).astype(f32)
+    small_lane, small_sub = iota(per_dev, 1), iota(per_dev, 0)
+
+    def column(mask, row):
+        return jnp.sum(jnp.where(mask, row, 0.0), axis=1, keepdims=True)
+
+    def as_row(col):
+        return jnp.sum(jnp.where(small_lane == small_sub, col, 0.0), axis=0, keepdims=True)
+
+    src_ids = column(own, src)
+    dst_ids = column(own, dst)
+    target = over(column(src_ids == dst, lane), per_dev)
+    same = (target == as_row(target)) & (small_lane < small_sub)
+    bucket = target * cap + column(same, 1.0)
+    slots = iota(send_index.shape[1], 1)
+    filled = jnp.where(bucket == slots, iota(send_index.shape[1], 0), 0.0)
+    send_index[...] = jnp.sum(filled, axis=0, keepdims=True).astype(jnp.int32)
+
+    root = column(dst_ids == src, lane)
+    owner = over(root, per_dev)
+    earlier = (owner == as_row(owner)) & (as_row(root) < root)
+    take_index[...] = as_row(owner * cap + column(earlier, 1.0)).astype(jnp.int32)
+
+    token, block = iota(per_dev * block_len, 1), iota(per_dev * block_len, 0)
+    holds = over(token, block_len) == block
+    ids = jnp.sum(jnp.where(holds, src_ids, 0.0), axis=0, keepdims=True)
+    inner = token[:1] - over(token[:1], block_len) * block_len
+    request = over(ids, per_request)
+    at = (ids - request * per_request) * block_len + inner
+    limit = jnp.zeros_like(at)
+    for r in range(REQS):
+        limit = jnp.where(request == r, lengths[r].astype(f32), limit)
+    tokens_of[...] = jnp.where(at < limit, request, -1.0).astype(jnp.int32)
+
+
+def plan(n, per_dev, block_len, src_blocks, dst_blocks, lengths):
+    total = src_blocks.shape[0]
+    slots = -(-n * ((per_dev + n - 1) // n) // HD) * HD
+    vmem = pl.BlockSpec(memory_space=pltpu.VMEM)
+    return pl.pallas_call(
+        functools.partial(plan_kernel, n, per_dev, block_len, total // REQS),
+        out_shape=(
+            jax.ShapeDtypeStruct((1, slots), jnp.int32),
+            jax.ShapeDtypeStruct((1, per_dev), jnp.int32),
+            jax.ShapeDtypeStruct((1, per_dev * block_len), jnp.int32),
+        ),
+        in_specs=[vmem, vmem, pl.BlockSpec(memory_space=pltpu.SMEM)],
+        out_specs=(vmem, vmem, vmem),
+        name="plan",
+    )(src_blocks.reshape(1, total), dst_blocks.reshape(1, total), lengths)
+
+
+def place_kernel(index, arrived, placed, held, in_sems, out_sems):
+    cap = arrived.shape[1]
+
+    def read(i):
+        at = index[0, i]
+        return pltpu.make_async_copy(
+            arrived.at[at // cap, lax.rem(at, cap)], held.at[i], in_sems.at[i]
+        )
+
+    def write(i):
+        return pltpu.make_async_copy(held.at[i], placed.at[i], out_sems.at[i])
+
+    def loop(body):
+        lax.fori_loop(0, held.shape[0], lambda i, c: (body(i), c)[1], 0)
+
+    loop(lambda i: read(i).start())
+    loop(lambda i: (read(i).wait(), write(i).start()))
+    loop(lambda i: write(i).wait())
+
+
+def place(arrived, index):
+    count = index.shape[1]
+    shape = (count,) + arrived.shape[2:]
+    dma = pltpu.SemaphoreType.DMA
+    return pl.pallas_call(
+        place_kernel,
+        out_shape=jax.ShapeDtypeStruct(shape, arrived.dtype),
+        in_specs=[pl.BlockSpec(memory_space=pltpu.SMEM), pl.BlockSpec(memory_space=pl.ANY)],
+        out_specs=pl.BlockSpec(memory_space=pl.ANY),
+        scratch_shapes=[pltpu.VMEM(shape, arrived.dtype), dma((count,)), dma((count,))],
+        compiler_params=pltpu.CompilerParams(vmem_limit_bytes=16 * 1024 * 1024),
+        name="place",
+    )(index, arrived)
+
+
 def split_bf16(value):
     high = value.astype(jnp.bfloat16)
     low = (value - high.astype(jnp.float32)).astype(jnp.bfloat16)
@@ -34,17 +137,16 @@
     groups,
     halves,
     send_index,
-    take_index,
     cache,
     queries,
     fresh_keys,
     fresh_values,
     token_request,
-    fresh_bias,
-    placed,
+    arrived,
     result,
     outgoing,
-    arrived,
+    fresh_rows,
+    fresh_bias,
     acc,
     acc_core,
     acc_near,
@@ -60,6 +162,7 @@
     pair_recv,
     far_send,
     far_recv,
+    own_sem,
 ):
     me = lax.axis_index("ctx")
     blocks, layers, _, block_len, _ = cache.shape
@@ -103,34 +206,87 @@
             outgoing.at[peer(k)], arrived.at[me], block_send.at[k], block_recv.at[k], peer(k)
         )
 
-    def send_blocks(k):
+    def fill(to):
         for c in range(cap):
-            outgoing[peer(k), c] = cache[send_index[peer(k) * cap + c]]
+            outgoing[to, c] = cache[send_index[0, to * cap + c]]
+
+    def shift(i):
+        j = i // 2
+        odd = lax.rem(j, 2)
+        far = n // 2 + odd * (j + 1) // 2 - (1 - odd) * (j // 2)
+        near = (1 - odd) * (1 + j // 2) + odd * (n - (j + 1) // 2)
+        pick = lax.rem(i, 2)
+        return (1 - pick) * far + pick * near
+
+    def send_blocks(i):
+        k = shift(i)
+        fill(peer(k))
         block_copy(k).start()
 
-    loop(1, n, send_blocks)
-    for c in range(cap):
-        arrived[me, c] = cache[send_index[me * cap + c]]
+    windows = [0, n * 5 // 16, n * 7 // 16, n * 10 // 16, n - 1]
+
+    def send_window(w):
+        loop(windows[w], windows[w + 1], send_blocks)
+
+    send_window(0)
+    fill(me)
+    own_copy = pltpu.make_async_copy(outgoing.at[me], arrived.at[me], own_sem.at[0])
+    own_copy.start()
+
+    steps = queries.shape[0]
+    heads = rows // steps
+    fresh = steps * REQS
+    for which, value in ((0, fresh_keys), (1, fresh_values)):
+        for layer in range(layers):
+            parts = [value[u, layer].astype(jnp.float32) for u in range(steps)]
+            parts.append(jnp.zeros((fresh_rows.shape[2] - fresh, KVH * HD), jnp.float32))
+            fresh_rows[which, layer] = jnp.concatenate(parts, axis=0).astype(jnp.bfloat16)
+    bias_shape = (width, fresh_rows.shape[2])
+    row = lax.broadcasted_iota(jnp.int32, bias_shape, 0)
+    col = lax.broadcasted_iota(jnp.int32, bias_shape, 1)
+    for h in range(1, halves):
+        row = jnp.where(row >= rows, row - rows, row)
+    row_step = sum((row >= heads * j).astype(jnp.int32) for j in range(1, steps))
+    col_step = sum((col >= REQS * j).astype(jnp.int32) for j in range(1, steps))
+    col_request = col - REQS * col_step
+    usable = (col_step <= row_step) & (col < fresh) & (me == 0)
+    for r in range(REQS):
+        fresh_bias[r * width : (r + 1) * width] = jnp.where(
+            usable & (col_request == r), 0.0, NEG_BIG
+        )
 
     stat_cols[...] = jnp.zeros_like(stat_cols)
     lane = lax.broadcasted_iota(jnp.int32, (1, HD), 1)
-    fresh_live = jnp.where(me == 0, 0.0, NEG_BIG)
+
+    def query_rows(layer, g):
+        span = pl.ds(pl.multiple_of(g * QPG * HD, QPG * HD), QPG * HD)
+        parts = [
+            queries[step, layer, :, span].astype(jnp.float32).reshape(REQS, QPG, HD)
+            for step in range(steps)
+        ]
+        ordered = [
+            parts[step][r, h * heads : (h + 1) * heads]
+            for r in range(REQS)
+            for h in range(halves)
+            for step in range(steps)
+        ]
+        return jnp.concatenate(ordered, axis=0).astype(jnp.bfloat16)
 
     def head(g):
         cols = pl.ds(pl.multiple_of(g * HD, HD), HD)
         for layer in range(layers):
-            q = queries[layer, g]
+            q = query_rows(layer, g)
             k_cache = cache[:, layer, 0, :, cols].reshape(tokens, HD)
             v_cache = cache[:, layer, 1, :, cols].reshape(tokens, HD)
-            k_new = fresh_keys[layer, :, cols]
-            v_new = fresh_values[layer, :, cols]
+            k_new = fresh_rows[0, layer, :, cols]
+            v_new = fresh_rows[1, layer, :, cols]
             scores = dot(q, k_cache, 1) * (HD**-0.5)
             new_scores = dot(q, k_new, 1) * (HD**-0.5)
             for r in range(REQS):
                 part = slice(r * width, (r + 1) * width)
                 live = jnp.where(token_request[...] == r, 0.0, NEG_BIG)
                 s = scores[part] + live
-                s_new = new_scores[part] + (fresh_bias[part] + fresh_live)
+                s_new = new_scores[part] + fresh_bias[part]
                 top = jnp.maximum(
                     jnp.max(s, axis=1, keepdims=True), jnp.max(s_new, axis=1, keepdims=True)
                 )
@@ -188,9 +344,10 @@
                     + acc_new[gi, layer] * factor[:rows, layers + layer : layers + layer + 1]
                 )
 
-    def swap(copies):
+    def swap(copies, window):
         for copy in copies:
             copy.start()
+        send_window(window)
         for copy in copies:
             copy.wait()
 
@@ -199,7 +356,8 @@
         [
             send(stat.at[1 - bit0], stat_core, pair_send.at[0], pair_recv.at[0], core),
             send(acc.at[1 - bit0], acc_core, pair_send.at[1], pair_recv.at[1], core),
-        ]
+        ],
+        1,
     )
 
     def join_core(i):
@@ -215,7 +373,8 @@
         [
             send(stat.at[bit0, 1 - bit1], stat_near, pair_send.at[2], pair_recv.at[2], near),
             send(acc.at[bit0, 1 - bit1], acc_near, pair_send.at[3], pair_recv.at[3], near),
-        ]
+        ],
+        2,
     )
     loop(
         0,
@@ -242,6 +401,7 @@
         )
 
     loop(1, quarter, lambda k: [copy.start() for copy in far_copies(k)])
+    send_window(3)
     stat_far[high] = stat[bit0, bit1, high]
     acc_far[high] = acc[bit0, bit1, high]
     loop(1, quarter, lambda k: [copy.wait() for copy in far_copies(k)])
@@ -262,43 +422,18 @@
                     step * share : (step + 1) * share
                 ]
 
+    own_copy.wait()
     loop(1, n, lambda k: block_copy(k).wait())
 
-    def place(j):
-        at = take_index[j]
-        placed[j] = arrived[at // cap, lax.rem(at, cap)]
-
-    loop(0, blocks, place)
-
-
-def exchange(n, cap, send_index, take_index, cache, queries, fresh_keys, fresh_values, token_request):
+
+def exchange(n, cap, send_index, cache, queries, fresh_keys, fresh_values, token_request):
     steps, layers, requests, _ = queries.shape
     share = requests * KVH * QPG // n
     groups = max(share // QPG, 1)
     halves = max(QPG // share, 1)
     heads = QPG // halves
     rows = steps * heads
-    q = queries.reshape(steps, layers, requests, KVH, halves, heads, HD)
-    q = jnp.transpose(q, (1, 3, 2, 4, 0, 5, 6)).reshape(
-        layers, KVH, requests * halves * rows, HD
-    )
-    fresh = steps * requests
-    fresh_pad = -(-fresh // 16) * 16
-
-    def fresh_rows(value):
-        value = jnp.transpose(value, (1, 0, 2, 3)).reshape(layers, fresh, KVH * HD)
-        return jnp.pad(value, ((0, 0), (0, fresh_pad - fresh), (0, 0)))
-
-    row = jnp.arange(requests * halves * rows)
-    row_request = row // (halves * rows)
-    row_step = row % rows // heads
-    col = jnp.arange(fresh_pad)
-    seen = (
-        (col[None, :] % requests == row_request[:, None])
-        & (col[None, :] // requests <= row_step[:, None])
-        & (col[None, :] < fresh)
-    )
-    fresh_bias = jnp.where(seen, 0.0, NEG_BIG).astype(jnp.float32)
+    fresh_pad = -(-steps * requests // 16) * 16
     quarter = n // 4
     block = cache.shape[1:]
     piece = (groups, layers, rows, HD)
@@ -310,14 +445,15 @@
     return pl.pallas_call(
         functools.partial(exchange_kernel, n, groups, halves),
         out_shape=(
-            jax.ShapeDtypeStruct(cache.shape, cache.dtype),
+            jax.ShapeDtypeStruct((n, cap) + block, cache.dtype),
             jax.ShapeDtypeStruct((steps, layers, share, HD), f32),
         ),
-        in_specs=[smem] * 2 + [vmem] * 6,
-        out_specs=(vmem, vmem),
+        in_specs=[smem] + [vmem] * 5,
+        out_specs=(pl.BlockSpec(memory_space=pl.ANY), vmem),
         scratch_shapes=[
             pltpu.VMEM((n, cap) + block, cache.dtype),
-            pltpu.VMEM((n, cap) + block, cache.dtype),
+            pltpu.VMEM((2, layers, fresh_pad, KVH * HD), cache.dtype),
+            pltpu.VMEM((requests * halves * rows, fresh_pad), f32),
             pltpu.VMEM((2, 2, quarter) + piece, f32),
             pltpu.VMEM((2, quarter) + piece, f32),
             pltpu.VMEM((quarter,) + piece, f32),
@@ -333,57 +469,26 @@
             dma((4,)),
             dma((2, quarter)),
             dma((2, quarter)),
+            dma((1,)),
         ],
         compiler_params=pltpu.CompilerParams(
             collective_id=0, has_side_effects=True, vmem_limit_bytes=56 * 1024 * 1024
         ),
         name="exchange",
-    )(
-        send_index,
-        take_index,
-        cache,
-        q,
-        fresh_rows(fresh_keys),
-        fresh_rows(fresh_values),
-        token_request,
-        fresh_bias,
-    )
+    )(send_index, cache, queries, fresh_keys, fresh_values, token_request)
 
 
 def local(src_cache, src_blocks, dst_blocks, ctx_lengths, queries, new_keys, new_values):
     n = lax.axis_size("ctx")
-    me = lax.axis_index("ctx")
     per_dev, _, _, block_len, _ = src_cache.shape
-    total = src_blocks.shape[0]
-    per_request = total // REQS
     cap = (per_dev + n - 1) // n
-    slots = jnp.arange(total, dtype=jnp.int32)
-    pos = jnp.arange(per_dev, dtype=jnp.int32)
-    src_ids = lax.dynamic_slice_in_dim(src_blocks, me * per_dev, per_dev)
-    dst_ids = lax.dynamic_slice_in_dim(dst_blocks, me * per_dev, per_dev)
-
-    target = jnp.sum(jnp.where(src_ids[:, None] == dst_blocks[None], slots[None], 0), axis=1) // per_dev
-    before = (target[:, None] == target[None]) & (pos[None] < pos[:, None])
-    bucket = target * cap + jnp.sum(before.astype(jnp.int32), axis=1)
-    bucket_ids = jnp.arange(n * cap, dtype=jnp.int32)
-    chosen = jnp.sum(jnp.where(bucket_ids[:, None] == bucket[None], pos[None], 0), axis=1)
-
-    root = jnp.sum(jnp.where(dst_ids[:, None] == src_blocks[None], slots[None], 0), axis=1)
-    owner = root // per_dev
-    earlier = (owner[:, None] == owner[None]) & (root[None] < root[:, None])
-    rows = owner * cap + jnp.sum(earlier.astype(jnp.int32), axis=1)
-
-    request = src_ids // per_request
-    limit = jnp.sum(
-        jnp.where(request[:, None] == jnp.arange(REQS)[None], ctx_lengths[None], 0), axis=1
-    )
-    at = (src_ids % per_request)[:, None] * block_len + jnp.arange(block_len)[None]
-    token_request = jnp.where(at < limit[:, None], request[:, None], -1).astype(jnp.int32)
-    token_request = token_request.reshape(1, per_dev * block_len)
-
-    return exchange(
-        n, cap, chosen, rows, src_cache, queries, new_keys, new_values, token_request
-    )
+    send_index, take_index, token_request = plan(
+        n, per_dev, block_len, src_blocks, dst_blocks, ctx_lengths
+    )
+    arrived, attn = exchange(
+        n, cap, send_index, src_cache, queries, new_keys, new_values, token_request
+    )
+    return place(arrived, take_index), attn
 
 
 def solution(mesh):

time: 139 us -> 128 us (0.921)
  local copies, waits for them, and re-layouts: 14.9 us -> 2.86 us
  Pallas kernels: 117 us -> 125 us
  other arithmetic: 5.84 us -> 0 us
    pallas_call x0 -> x2, Pallas kernels: none -> 10.7 us  [the longest x1 8.98 us: place(): pl.pallas_call(place_kernel, out_shape=jax.ShapeDtypeStruct(shape, arrive...]
    reshape x4 -> x0, local copies, waits for them, and re-layouts: 4.47 us -> none  [the longest x2 4.44 us: exchange(): q = queries.reshape(steps, layers, requests, KVH, halves, heads, HD)]
    reduce_sum x6 -> x0, other arithmetic: 3.51 us -> none  [the longest x1 0.87 us: local(): jnp.sum(jnp.where(src_ids[:, None] == dst_blocks[None], slots[None], 0),...]
    unnamed x4 -> x7, local copies, waits for them, and re-layouts: 5.75 us -> 2.86 us
    pallas_call x1, Pallas kernels: 117 us -> 114 us  [exchange(): pl.pallas_call(functools.partial(exchange_kernel, n, groups, halves), out...]
    transpose x2 -> x0, local copies, waits for them, and re-layouts: 1.9 us -> none  [fresh_rows(): value = jnp.transpose(value, (1, 0, 2, 3)).reshape(layers, fresh, KVH * HD)]
where the time goes in v3:
time: 128 us
  Pallas kernels  125 us (98%)
  local copies, waits for them, and re-layouts  2.86 us (2%)
    pallas_call x1, Pallas kernels, exchange(): pl.pallas_call(functools.partial(exchange_kernel, n, groups, halves), out...  114 us
    pallas_call x1, Pallas kernels, place(): pl.pallas_call(place_kernel, out_shape=jax.ShapeDtypeStruct(shape, arrive...  8.98 us
    unnamed x7, local copies, waits for them, and re-layouts  2.86 us

profile of v3, /device:TPU:9, one launch (start us, length us, event | category | flops | bytes accessed | tf_op | source)
XLA Modules:
  0.0 128.2 jit_solution(17829347069816638526)
XLA Ops:
  0.6 1.7 %plan.1 = (s32[1,128]{1,0:T(1,128)}, s32[1,32]{1,0:T(1,128)}, s32[1,512]{1,0:T(1,128)}) custom-call(s32[1,512]{1,0:T(1,128)} %bitcast.2, s32[1,512]{1,0:T(1,128)} %bitcast.3, s32[4]{0:T(128)} %lengths.1), custom_call_target="tpu_custom_call" | custom-call | tf_op jit(solution)/shard_map/plan/pallas_call | solution.py:75
  2.3 0.0 copy-start.1
  2.3 114.0 %exchange.1 = (bf16[16,2,2,2,16,1024]{5,4,3,2,1,0:T(8,128)(2,1)}, f32[5,2,32,128]{3,2,1,0:T(8,128)}) custom-call(s32[1,128]{1,0:T(1,128)} %get-tuple-element.8.send_index, bf16[32,2,2,16,1024]{4,3,2,1,0:T(8,128)(2,1)} %cache.1, bf16[5,2,4,16384]{3,2,1,0:T(4,128)(2,1)} %queries.1, bf16[5,2,4,1024]{3,2,1,0:T(4,128)(2,1)} %fresh_keys.1, ...), custom_call_target="tpu_custom_call" | custom-call | tf_op jit(solution)/shard_map/exchange/pallas_call | solution.py:445
  116.3 0.0 copy-done.1
  116.3 0.0 copy-start
  116.3 2.2 %copy-done = bf16[16,2,2,2,16,1024]{5,4,3,2,1,0:T(8,128)(2,1)S(1)} copy-done((bf16[16,2,2,2,16,1024]{5,4,3,2,1,0:T(8,128)(2,1)S(1)}, bf16[16,2,2,2,16,1024]{5,4,3,2,1,0:T(8,128)(2,1)}, u32[]{:S(2)}) %copy-start) | copy-done | bytes 4194328
  118.5 0.0 copy-start.2
  118.5 9.0 %place.1 = bf16[32,2,2,16,1024]{4,3,2,1,0:T(8,128)(2,1)} custom-call(s32[1,32]{1,0:T(1,128)S(1)} %copy-done.1, bf16[16,2,2,2,16,1024]{5,4,3,2,1,0:T(8,128)(2,1)S(1)} %copy-done), custom_call_target="tpu_custom_call" | custom-call | tf_op jit(solution)/shard_map/place/pallas_call | solution.py:112
  127.5 0.0 copy-done.2
  127.5 0.7 copy.10
Async XLA Ops:
  2.3 114.0 %copy-start.1 = (s32[1,32]{1,0:T(1,128)S(1)}, s32[1,32]{1,0:T(1,128)}, u32[]{:S(2)}) copy-start(s32[1,32]{1,0:T(1,128)} %get-tuple-element.7.index) | copy-start | bytes 388
  116.3 2.2 %copy-start = (bf16[16,2,2,2,16,1024]{5,4,3,2,1,0:T(8,128)(2,1)S(1)}, bf16[16,2,2,2,16,1024]{5,4,3,2,1,0:T(8,128)(2,1)}, u32[]{:S(2)}) copy-start(bf16[16,2,2,2,16,1024]{5,4,3,2,1,0:T(8,128)(2,1)} %get-tuple-element.10.arrived) | copy-start | bytes 12582916
  118.5 9.0 %copy-start.2 = (f32[5,2,32,128]{3,2,1,0:T(8,128)S(1)}, f32[5,2,32,128]{3,2,1,0:T(8,128)}, u32[]{:S(2)}) copy-start(f32[5,2,32,128]{3,2,1,0:T(8,128)} %get-tuple-element.15) | copy-start | bytes 491524

commit v4 on v3

--- a/solution.py
+++ b/solution.py
@@ -85,7 +85,9 @@
     )(src_blocks.reshape(1, total), dst_blocks.reshape(1, total), lengths)
 
 
-def place_kernel(index, arrived, placed, held, in_sems, out_sems):
+def place_kernel(
+    index, arrived, attn, placed, result, held, held_attn, in_sems, out_sems, attn_sems
+):
     cap = arrived.shape[1]
 
     def read(i):
@@ -100,24 +102,40 @@
     def loop(body):
         lax.fori_loop(0, held.shape[0], lambda i, c: (body(i), c)[1], 0)
 
+    attn_in = pltpu.make_async_copy(attn, held_attn, attn_sems.at[0])
+    attn_out = pltpu.make_async_copy(held_attn, result, attn_sems.at[1])
+    attn_in.start()
     loop(lambda i: read(i).start())
+    attn_in.wait()
+    attn_out.start()
     loop(lambda i: (read(i).wait(), write(i).start()))
     loop(lambda i: write(i).wait())
-
-
-def place(arrived, index):
+    attn_out.wait()
+
+
+def place(arrived, attn, index):
     count = index.shape[1]
     shape = (count,) + arrived.shape[2:]
     dma = pltpu.SemaphoreType.DMA
+    hbm = pl.BlockSpec(memory_space=pl.ANY)
     return pl.pallas_call(
         place_kernel,
-        out_shape=jax.ShapeDtypeStruct(shape, arrived.dtype),
-        in_specs=[pl.BlockSpec(memory_space=pltpu.SMEM), pl.BlockSpec(memory_space=pl.ANY)],
-        out_specs=pl.BlockSpec(memory_space=pl.ANY),
-        scratch_shapes=[pltpu.VMEM(shape, arrived.dtype), dma((count,)), dma((count,))],
-        compiler_params=pltpu.CompilerParams(vmem_limit_bytes=16 * 1024 * 1024),
+        out_shape=(
+            jax.ShapeDtypeStruct(shape, arrived.dtype),
+            jax.ShapeDtypeStruct(attn.shape, attn.dtype),
+        ),
+        in_specs=[pl.BlockSpec(memory_space=pltpu.SMEM), hbm, hbm],
+        out_specs=(hbm, hbm),
+        scratch_shapes=[
+            pltpu.VMEM(shape, arrived.dtype),
+            pltpu.VMEM(attn.shape, attn.dtype),
+            dma((count,)),
+            dma((count,)),
+            dma((2,)),
+        ],
+        compiler_params=pltpu.CompilerParams(vmem_limit_bytes=60 * 1024 * 1024),
         name="place",
-    )(index, arrived)
+    )(index, arrived, attn)
 
 
 def split_bf16(value):
@@ -137,13 +155,15 @@
     groups,
     halves,
     send_index,
-    cache,
-    queries,
+    cache_ref,
+    queries_ref,
     fresh_keys,
     fresh_values,
     token_request,
     arrived,
     result,
+    cache,
+    queries,
     outgoing,
     fresh_rows,
     fresh_bias,
@@ -191,6 +211,11 @@
             device_id_type=MESH,
         )
 
+    cache_load = pltpu.make_async_copy(cache_ref, cache, own_sem.at[1])
+    queries_load = pltpu.make_async_copy(queries_ref, queries, own_sem.at[2])
+    cache_load.start()
+    queries_load.start()
+
     barrier = pltpu.get_barrier_semaphore()
     loop(
         1,
@@ -200,6 +225,7 @@
         ),
     )
     pl.semaphore_wait(barrier, n - 1)
+    cache_load.wait()
 
     def block_copy(k):
         return send(
@@ -223,7 +249,7 @@
         fill(peer(k))
         block_copy(k).start()
 
-    windows = [0, n * 5 // 16, n * 7 // 16, n * 10 // 16, n - 1]
+    windows = [0, n // 4, n // 2, n * 5 // 8, n * 3 // 4, n - 1]
 
     def send_window(w):
         loop(windows[w], windows[w + 1], send_blocks)
@@ -310,7 +336,19 @@
                 now = jnp.where(lane == at, top, now)
                 stat_cols[part] = jnp.where(lane == at + layers, total, now)
 
-    loop(0, KVH, head)
+    queries_load.wait()
+    span = windows[2] - windows[1]
+    stops = KVH // 2
+
+    def head_pair(i):
+        loop(2 * i, 2 * i + 2, head)
+        loop(
+            windows[1] + lax.div(span * i, stops),
+            windows[1] + lax.div(span * (i + 1), stops),
+            send_blocks,
+        )
+
+    loop(0, stops, head_pair)
 
     pad = jnp.zeros((HD - rows, HD), jnp.float32)
     for r in range(REQS):
@@ -357,7 +395,7 @@
             send(stat.at[1 - bit0], stat_core, pair_send.at[0], pair_recv.at[0], core),
             send(acc.at[1 - bit0], acc_core, pair_send.at[1], pair_recv.at[1], core),
         ],
-        1,
+        2,
     )
 
     def join_core(i):
@@ -374,7 +412,7 @@
             send(stat.at[bit0, 1 - bit1], stat_near, pair_send.at[2], pair_recv.at[2], near),
             send(acc.at[bit0, 1 - bit1], acc_near, pair_send.at[3], pair_recv.at[3], near),
         ],
-        2,
+        3,
     )
     loop(
         0,
@@ -401,7 +439,7 @@
         )
 
     loop(1, quarter, lambda k: [copy.start() for copy in far_copies(k)])
-    send_window(3)
+    send_window(4)
     stat_far[high] = stat[bit0, bit1, high]
     acc_far[high] = acc[bit0, bit1, high]
     loop(1, quarter, lambda k: [copy.wait() for copy in far_copies(k)])
@@ -440,6 +478,7 @@
     note = (groups, STAT_ROWS, HD)
     vmem = pl.BlockSpec(memory_space=pltpu.VMEM)
     smem = pl.BlockSpec(memory_space=pltpu.SMEM)
+    hbm = pl.BlockSpec(memory_space=pl.ANY)
     dma = pltpu.SemaphoreType.DMA
     f32 = jnp.float32
     return pl.pallas_call(
@@ -448,9 +487,11 @@
             jax.ShapeDtypeStruct((n, cap) + block, cache.dtype),
             jax.ShapeDtypeStruct((steps, layers, share, HD), f32),
         ),
-        in_specs=[smem] + [vmem] * 5,
-        out_specs=(pl.BlockSpec(memory_space=pl.ANY), vmem),
+        in_specs=[smem, hbm, hbm] + [vmem] * 3,
+        out_specs=(hbm, vmem),
         scratch_shapes=[
+            pltpu.VMEM(cache.shape, cache.dtype),
+            pltpu.VMEM(queries.shape, queries.dtype),
             pltpu.VMEM((n, cap) + block, cache.dtype),
             pltpu.VMEM((2, layers, fresh_pad, KVH * HD), cache.dtype),
             pltpu.VMEM((requests * halves * rows, fresh_pad), f32),
@@ -469,7 +510,7 @@
             dma((4,)),
             dma((2, quarter)),
             dma((2, quarter)),
-            dma((1,)),
+            dma((3,)),
         ],
         compiler_params=pltpu.CompilerParams(
             collective_id=0, has_side_effects=True, vmem_limit_bytes=56 * 1024 * 1024
@@ -488,7 +529,7 @@
     arrived, attn = exchange(
         n, cap, send_index, src_cache, queries, new_keys, new_values, token_request
     )
-    return place(arrived, take_index), attn
+    return place(arrived, attn, take_index)
 
 
 def solution(mesh):

time: 128 us -> 120 us (0.938)
  Pallas kernels: 125 us -> 119 us
  local copies, waits for them, and re-layouts: 2.86 us -> 0 us
    pallas_call x1, Pallas kernels: 8.98 us -> 5.42 us  [place(): pl.pallas_call(place_kernel, out_shape=(jax.ShapeDtypeStruct(shape, arriv...]
    unnamed x7 -> x0, local copies, waits for them, and re-layouts: 2.86 us -> none
    pallas_call x1, Pallas kernels: 114 us -> 112 us  [exchange(): pl.pallas_call(functools.partial(exchange_kernel, n, groups, halves), out...]
where the time goes in v4:
time: 120 us
  Pallas kernels  119 us (99%)
    pallas_call x1, Pallas kernels, exchange(): pl.pallas_call(functools.partial(exchange_kernel, n, groups, halves), out...  112 us
    pallas_call x1, Pallas kernels, place(): pl.pallas_call(place_kernel, out_shape=(jax.ShapeDtypeStruct(shape, arriv...  5.42 us

profile of v4, /device:TPU:9, one launch (start us, length us, event | category | flops | bytes accessed | tf_op | source)
XLA Modules:
  0.0 120.0 jit_solution(15293065438992064076)
XLA Ops:
  0.6 1.7 %plan.1 = (s32[1,128]{1,0:T(1,128)}, s32[1,32]{1,0:T(1,128)}, s32[1,512]{1,0:T(1,128)}) custom-call(s32[1,512]{1,0:T(1,128)} %bitcast.2, s32[1,512]{1,0:T(1,128)} %bitcast.3, s32[4]{0:T(128)} %lengths.1), custom_call_target="tpu_custom_call" | custom-call | tf_op jit(solution)/shard_map/plan/pallas_call | solution.py:75
  2.3 112.3 %exchange.1 = (bf16[16,2,2,2,16,1024]{5,4,3,2,1,0:T(8,128)(2,1)}, f32[5,2,32,128]{3,2,1,0:T(8,128)}) custom-call(s32[1,128]{1,0:T(1,128)} %get-tuple-element.8.send_index, bf16[32,2,2,16,1024]{4,3,2,1,0:T(8,128)(2,1)} %cache_ref.1, bf16[5,2,4,16384]{3,2,1,0:T(4,128)(2,1)} %queries_ref.1, bf16[5,2,4,1024]{3,2,1,0:T(4,128)(2,1)} %fresh_keys.1, ...), custom_call_target="tpu_custom_call" | custom-call | tf_op jit(solution)/shard_map/exchange/pallas_call | solution.py:484
  114.6 5.4 %place.1 = (bf16[32,2,2,16,1024]{4,3,2,1,0:T(8,128)(2,1)}, f32[5,2,32,128]{3,2,1,0:T(8,128)}) custom-call(s32[1,32]{1,0:T(1,128)} %get-tuple-element.7.index, bf16[16,2,2,2,16,1024]{5,4,3,2,1,0:T(8,128)(2,1)} %get-tuple-element.10.arrived, f32[5,2,32,128]{3,2,1,0:T(8,128)} %get-tuple-element.11.attn), custom_call_target="tpu_custom_call" | custom-call | tf_op jit(solution)/shard_map/place/pallas_call | solution.py:121

commit v5 on v4

--- a/solution.py
+++ b/solution.py
@@ -85,30 +85,21 @@
     )(src_blocks.reshape(1, total), dst_blocks.reshape(1, total), lengths)
 
 
-def place_kernel(
-    index, arrived, attn, placed, result, held, held_attn, in_sems, out_sems, attn_sems
-):
+def place_kernel(index, arrived, attn, placed, result, sems, attn_sem):
     cap = arrived.shape[1]
 
-    def read(i):
+    def write(i):
         at = index[0, i]
         return pltpu.make_async_copy(
-            arrived.at[at // cap, lax.rem(at, cap)], held.at[i], in_sems.at[i]
-        )
-
-    def write(i):
-        return pltpu.make_async_copy(held.at[i], placed.at[i], out_sems.at[i])
+            arrived.at[at // cap, lax.rem(at, cap)], placed.at[i], sems.at[i]
+        )
 
     def loop(body):
-        lax.fori_loop(0, held.shape[0], lambda i, c: (body(i), c)[1], 0)
-
-    attn_in = pltpu.make_async_copy(attn, held_attn, attn_sems.at[0])
-    attn_out = pltpu.make_async_copy(held_attn, result, attn_sems.at[1])
-    attn_in.start()
-    loop(lambda i: read(i).start())
-    attn_in.wait()
+        lax.fori_loop(0, placed.shape[0], lambda i, c: (body(i), c)[1], 0)
+
+    attn_out = pltpu.make_async_copy(attn, result, attn_sem.at[0])
+    loop(lambda i: write(i).start())
     attn_out.start()
-    loop(lambda i: (read(i).wait(), write(i).start()))
     loop(lambda i: write(i).wait())
     attn_out.wait()
 
@@ -118,22 +109,20 @@
     shape = (count,) + arrived.shape[2:]
     dma = pltpu.SemaphoreType.DMA
     hbm = pl.BlockSpec(memory_space=pl.ANY)
+    vmem = pl.BlockSpec(memory_space=pltpu.VMEM)
     return pl.pallas_call(
         place_kernel,
         out_shape=(
             jax.ShapeDtypeStruct(shape, arrived.dtype),
             jax.ShapeDtypeStruct(attn.shape, attn.dtype),
         ),
-        in_specs=[pl.BlockSpec(memory_space=pltpu.SMEM), hbm, hbm],
+        in_specs=[pl.BlockSpec(memory_space=pltpu.SMEM), vmem, vmem],
         out_specs=(hbm, hbm),
         scratch_shapes=[
-            pltpu.VMEM(shape, arrived.dtype),
-            pltpu.VMEM(attn.shape, attn.dtype),
             dma((count,)),
-            dma((count,)),
-            dma((2,)),
+            dma((1,)),
         ],
-        compiler_params=pltpu.CompilerParams(vmem_limit_bytes=60 * 1024 * 1024),
+        compiler_params=pltpu.CompilerParams(vmem_limit_bytes=16 * 1024 * 1024),
         name="place",
     )(index, arrived, attn)
 
@@ -155,51 +144,43 @@
     groups,
     halves,
     send_index,
-    cache_ref,
-    queries_ref,
+    cache,
+    queries,
     fresh_keys,
     fresh_values,
     token_request,
     arrived,
     result,
-    cache,
-    queries,
     outgoing,
     fresh_rows,
     fresh_bias,
     acc,
-    acc_core,
-    acc_near,
-    acc_far,
+    acc_in,
     stat,
-    stat_core,
-    stat_near,
-    stat_far,
+    stat_in,
     stat_cols,
     block_send,
     block_recv,
     pair_send,
     pair_recv,
-    far_send,
-    far_recv,
     own_sem,
 ):
     me = lax.axis_index("ctx")
     blocks, layers, _, block_len, _ = cache.shape
     tokens = blocks * block_len
     cap = outgoing.shape[1]
-    quarter = n // 4
-    rows = acc.shape[5]
+    rows = acc.shape[3]
+    stages = n.bit_length() - 1
     width = rows * halves
-    bit0 = lax.rem(me, 2)
-    bit1 = lax.rem(me // 2, 2)
-    high = me // 4
 
     def loop(start, stop, body):
         lax.fori_loop(start, stop, lambda k, c: (body(k), c)[1], 0)
 
     def peer(k):
         return lax.rem(me + k, n)
+
+    def place_of(to):
+        return sum(to // 2**j % 2 * (n // 2 ** (j + 1)) for j in range(stages))
 
     def send(src, dst, send_sem, recv_sem, device):
         return pltpu.make_async_remote_copy(
@@ -211,11 +192,6 @@
             device_id_type=MESH,
         )
 
-    cache_load = pltpu.make_async_copy(cache_ref, cache, own_sem.at[1])
-    queries_load = pltpu.make_async_copy(queries_ref, queries, own_sem.at[2])
-    cache_load.start()
-    queries_load.start()
-
     barrier = pltpu.get_barrier_semaphore()
     loop(
         1,
@@ -225,7 +201,6 @@
         ),
     )
     pl.semaphore_wait(barrier, n - 1)
-    cache_load.wait()
 
     def block_copy(k):
         return send(
@@ -249,7 +224,10 @@
         fill(peer(k))
         block_copy(k).start()
 
-    windows = [0, n // 4, n // 2, n * 5 // 8, n * 3 // 4, n - 1]
+    rest = n // 2
+    windows = [0, n // 4] + [
+        rest + (n - 1 - rest) * j // stages for j in range(stages + 1)
+    ]
 
     def send_window(w):
         loop(windows[w], windows[w + 1], send_blocks)
@@ -329,14 +307,13 @@
                 )
                 for h in range(halves):
                     chunk = (r * KVH + g) * halves + h
-                    to, gi = chunk // groups, chunk % groups
-                    acc[to % 2, to // 2 % 2, to // 4, gi, layer] = sums[h * rows : (h + 1) * rows]
+                    at = place_of(chunk // groups)
+                    acc[at, chunk % groups, layer] = sums[h * rows : (h + 1) * rows]
                 at = g * STAT_ROWS + layer
                 now = stat_cols[part]
                 now = jnp.where(lane == at, top, now)
                 stat_cols[part] = jnp.where(lane == at + layers, total, now)
 
-    queries_load.wait()
     span = windows[2] - windows[1]
     stops = KVH // 2
 
@@ -357,8 +334,7 @@
             turned = jnp.concatenate([stat_cols[start : start + rows], pad], axis=0).T
             for g in range(KVH):
                 chunk = (r * KVH + g) * halves + h
-                to, gi = chunk // groups, chunk % groups
-                stat[to % 2, to // 2 % 2, to // 4, gi] = turned[
+                stat[place_of(chunk // groups), chunk % groups] = turned[
                     g * STAT_ROWS : (g + 1) * STAT_ROWS
                 ]
 
@@ -382,79 +358,43 @@
                     + acc_new[gi, layer] * factor[:rows, layers + layer : layers + layer + 1]
                 )
 
-    def swap(copies, window):
+    base = 0
+    for stage in range(stages):
+        half = n // 2 ** (stage + 1)
+        bit = lax.rem(me // 2**stage, 2)
+        partner = me + 2**stage * (1 - 2 * bit)
+        keep, give = base + bit * half, base + (1 - bit) * half
+        at = n - 2 * half
+        copies = [
+            send(
+                src.at[pl.ds(give, half)],
+                dst.at[pl.ds(at, half)],
+                pair_send.at[i, stage],
+                pair_recv.at[i, stage],
+                partner,
+            )
+            for i, (src, dst) in enumerate(((stat, stat_in), (acc, acc_in)))
+        ]
         for copy in copies:
             copy.start()
-        send_window(window)
+        loop(windows[2 + stage], windows[3 + stage], send_blocks)
         for copy in copies:
             copy.wait()
-
-    core = me + 1 - 2 * bit0
-    swap(
-        [
-            send(stat.at[1 - bit0], stat_core, pair_send.at[0], pair_recv.at[0], core),
-            send(acc.at[1 - bit0], acc_core, pair_send.at[1], pair_recv.at[1], core),
-        ],
-        2,
-    )
-
-    def join_core(i):
-        b, z = i // quarter, lax.rem(i, quarter)
-        join(
-            acc.at[bit0, b, z], stat.at[bit0, b, z], acc_core.at[b, z], stat_core.at[b, z]
-        )
-
-    loop(0, 2 * quarter, join_core)
-
-    near = me + 2 - 4 * bit1
-    swap(
-        [
-            send(stat.at[bit0, 1 - bit1], stat_near, pair_send.at[2], pair_recv.at[2], near),
-            send(acc.at[bit0, 1 - bit1], acc_near, pair_send.at[3], pair_recv.at[3], near),
-        ],
-        3,
-    )
-    loop(
-        0,
-        quarter,
-        lambda z: join(
-            acc.at[bit0, bit1, z], stat.at[bit0, bit1, z], acc_near.at[z], stat_near.at[z]
-        ),
-    )
-
-    def far_copies(k):
-        to = lax.rem(high + k, quarter)
-        device = to * 4 + lax.rem(me, 4)
-        return (
-            send(
-                stat.at[bit0, bit1, to],
-                stat_far.at[high],
-                far_send.at[0, k],
-                far_recv.at[0, k],
-                device,
+        loop(
+            0,
+            half,
+            lambda i, keep=keep, at=at: join(
+                acc.at[keep + i], stat.at[keep + i], acc_in.at[at + i], stat_in.at[at + i]
             ),
-            send(
-                acc.at[bit0, bit1, to], acc_far.at[high], far_send.at[1, k], far_recv.at[1, k], device
-            ),
-        )
-
-    loop(1, quarter, lambda k: [copy.start() for copy in far_copies(k)])
-    send_window(4)
-    stat_far[high] = stat[bit0, bit1, high]
-    acc_far[high] = acc[bit0, bit1, high]
-    loop(1, quarter, lambda k: [copy.wait() for copy in far_copies(k)])
+        )
+        base = keep
 
     share = rows // result.shape[0]
     for gi in range(groups):
+        totals = stat[base, gi, layers : 2 * layers]
+        factor = columns(1.0 / totals)
         for layer in range(layers):
-            tops = stat_far[:, gi, layer, :]
-            top = jnp.max(tops, axis=0, keepdims=True)
-            factor = jnp.exp(tops - top)
-            total = jnp.sum(factor * stat_far[:, gi, layers + layer, :], axis=0, keepdims=True)
-            factor = columns(factor / total)
-            out = jnp.zeros((rows, HD), jnp.float32)
-            for src in range(quarter):
-                out = out + factor[:rows, src : src + 1] * acc_far[src, gi, layer]
+            out = acc[base, gi, layer] * factor[:rows, layer : layer + 1]
             for step in range(result.shape[0]):
                 result[step, layer, gi * share : (gi + 1) * share, :] = out[
                     step * share : (step + 1) * share
@@ -472,7 +412,7 @@
     heads = QPG // halves
     rows = steps * heads
     fresh_pad = -(-steps * requests // 16) * 16
-    quarter = n // 4
+    stages = n.bit_length() - 1
     block = cache.shape[1:]
     piece = (groups, layers, rows, HD)
     note = (groups, STAT_ROWS, HD)
@@ -487,33 +427,25 @@
             jax.ShapeDtypeStruct((n, cap) + block, cache.dtype),
             jax.ShapeDtypeStruct((steps, layers, share, HD), f32),
         ),
-        in_specs=[smem, hbm, hbm] + [vmem] * 3,
+        in_specs=[smem] + [vmem] * 5,
         out_specs=(hbm, vmem),
         scratch_shapes=[
-            pltpu.VMEM(cache.shape, cache.dtype),
-            pltpu.VMEM(queries.shape, queries.dtype),
             pltpu.VMEM((n, cap) + block, cache.dtype),
             pltpu.VMEM((2, layers, fresh_pad, KVH * HD), cache.dtype),
             pltpu.VMEM((requests * halves * rows, fresh_pad), f32),
-            pltpu.VMEM((2, 2, quarter) + piece, f32),
-            pltpu.VMEM((2, quarter) + piece, f32),
-            pltpu.VMEM((quarter,) + piece, f32),
-            pltpu.VMEM((quarter,) + piece, f32),
-            pltpu.VMEM((2, 2, quarter) + note, f32),
-            pltpu.VMEM((2, quarter) + note, f32),
-            pltpu.VMEM((quarter,) + note, f32),
-            pltpu.VMEM((quarter,) + note, f32),
+            pltpu.VMEM((n,) + piece, f32),
+            pltpu.VMEM((n - 1,) + piece, f32),
+            pltpu.VMEM((n,) + note, f32),
+            pltpu.VMEM((n - 1,) + note, f32),
             pltpu.VMEM((requests * halves * rows, HD), f32),
             dma((n,)),
             dma((n,)),
-            dma((4,)),
-            dma((4,)),
-            dma((2, quarter)),
-            dma((2, quarter)),
-            dma((3,)),
+            dma((2, stages)),
+            dma((2, stages)),
+            dma((1,)),
         ],
         compiler_params=pltpu.CompilerParams(
-            collective_id=0, has_side_effects=True, vmem_limit_bytes=56 * 1024 * 1024
+            collective_id=0, has_side_effects=True, vmem_limit_bytes=32 * 1024 * 1024
         ),
         name="exchange",
     )(send_index, cache, queries, fresh_keys, fresh_values, token_request)

time: 120 us -> 117 us (0.975)
  the two profiles are of different devices: /device:TPU:9 before, /device:TPU:0 now
where the time goes in v5:
time: 117 us
  Pallas kernels  110 us (94%)
  local copies, waits for them, and re-layouts  6.62 us (6%)
    pallas_call x1, Pallas kernels, exchange(): pl.pallas_call(functools.partial(exchange_kernel, n, groups, halves), out...  105 us
    unnamed x14, local copies, waits for them, and re-layouts  6.62 us
    pallas_call x1, Pallas kernels, place(): pl.pallas_call(place_kernel, out_shape=(jax.ShapeDtypeStruct(shape, arriv...  2.88 us

profile of v5, /device:TPU:0, one launch (start us, length us, event | category | flops | bytes accessed | tf_op | source)
XLA Modules:
  0.0 117.1 jit_solution(5444600691466528060)
XLA Ops:
  0.6 1.7 %plan.1 = (s32[1,128]{1,0:T(1,128)}, s32[1,32]{1,0:T(1,128)}, s32[1,512]{1,0:T(1,128)}) custom-call(s32[1,512]{1,0:T(1,128)} %bitcast.2, s32[1,512]{1,0:T(1,128)} %bitcast.3, s32[4]{0:T(128)} %lengths.1), custom_call_target="tpu_custom_call" | custom-call | tf_op jit(solution)/shard_map/plan/pallas_call | solution.py:75
  2.3 0.0 copy-start.5
  2.3 0.0 copy-start
  2.3 2.2 %copy-done = bf16[32,2,2,16,1024]{4,3,2,1,0:T(8,128)(2,1)S(1)} copy-done((bf16[32,2,2,16,1024]{4,3,2,1,0:T(8,128)(2,1)S(1)}, bf16[32,2,2,16,1024]{4,3,2,1,0:T(8,128)(2,1)}, u32[]{:S(2)}) %copy-start) | copy-done | bytes 4194328
  4.5 0.0 copy-start.1
  4.5 1.3 %copy-done.1 = bf16[5,2,4,16384]{3,2,1,0:T(4,128)(2,1)S(1)} copy-done((bf16[5,2,4,16384]{3,2,1,0:T(4,128)(2,1)S(1)}, bf16[5,2,4,16384]{3,2,1,0:T(4,128)(2,1)}, u32[]{:S(2)}) %copy-start.1) | copy-done | bytes 1310744
  5.8 0.0 copy-start.2
  5.8 0.9 copy-done.2
  6.7 0.0 copy-start.3
  6.7 0.9 copy-done.3
  7.6 0.0 copy-start.4
  7.6 0.7 copy-done.4
  8.3 0.0 copy-start.6
  8.3 0.7 copy-done.6
  8.9 105.3 %exchange.1 = (bf16[16,2,2,2,16,1024]{5,4,3,2,1,0:T(8,128)(2,1)S(1)}, f32[5,2,32,128]{3,2,1,0:T(8,128)S(1)}) custom-call(s32[1,128]{1,0:T(1,128)S(1)} %copy-done.6, bf16[32,2,2,16,1024]{4,3,2,1,0:T(8,128)(2,1)S(1)} %copy-done, bf16[5,2,4,16384]{3,2,1,0:T(4,128)(2,1)S(1)} %copy-done.1, bf16[5,2,4,1024]{3,2,1,0:T(4,128)(2,1)S(1)} %copy-done.2, ...), custom_call_target="tpu_custom_call" | custom-call | tf_op jit(solution)/shard_map/exchange/pallas_call | solution.py:424
  114.2 0.0 copy-done.5
  114.2 2.9 %place.1 = (bf16[32,2,2,16,1024]{4,3,2,1,0:T(8,128)(2,1)}, f32[5,2,32,128]{3,2,1,0:T(8,128)}) custom-call(s32[1,32]{1,0:T(1,128)S(1)} %copy-done.5, bf16[16,2,2,2,16,1024]{5,4,3,2,1,0:T(8,128)(2,1)S(1)} %get-tuple-element.10.arrived, f32[5,2,32,128]{3,2,1,0:T(8,128)S(1)} %get-tuple-element.11.attn), custom_call_target="tpu_custom_call" | custom-call | tf_op jit(solution)/shard_map/place/pallas_call | solution.py:113
Async XLA Ops:
  2.3 111.9 %copy-start.5 = (s32[1,32]{1,0:T(1,128)S(1)}, s32[1,32]{1,0:T(1,128)}, u32[]{:S(2)}) copy-start(s32[1,32]{1,0:T(1,128)} %get-tuple-element.7.index) | copy-start | bytes 388
  2.3 2.2 %copy-start = (bf16[32,2,2,16,1024]{4,3,2,1,0:T(8,128)(2,1)S(1)}, bf16[32,2,2,16,1024]{4,3,2,1,0:T(8,128)(2,1)}, u32[]{:S(2)}) copy-start(bf16[32,2,2,16,1024]{4,3,2,1,0:T(8,128)(2,1)} %cache.1) | copy-start | bytes 12582916
  4.5 1.3 %copy-start.1 = (bf16[5,2,4,16384]{3,2,1,0:T(4,128)(2,1)S(1)}, bf16[5,2,4,16384]{3,2,1,0:T(4,128)(2,1)}, u32[]{:S(2)}) copy-start(bf16[5,2,4,16384]{3,2,1,0:T(4,128)(2,1)} %queries.1) | copy-start | bytes 3932164
  5.8 0.9 copy-start.2
  6.7 0.9 copy-start.3
  7.6 0.7 copy-start.4
  8.3 0.7 copy-start.6

commit v6 on v5

--- a/solution.py
+++ b/solution.py
@@ -17,89 +17,77 @@
 MESH = pl.DeviceIdType.MESH
 
 
-def plan_kernel(
-    n, per_dev, block_len, per_request, src_ref, dst_ref, lengths, send_index, take_index, tokens_of
-):
-    me = lax.axis_index("ctx")
+def over(value, by):
+    assert by & (by - 1) == 0
+    return lax.shift_right_logical(value, by.bit_length() - 1)
+
+
+def plan(n, me, per_dev, block_len, src, dst, lengths, send_index, take_index, tokens_of):
     cap = (per_dev + n - 1) // n
-    total = src_ref.shape[1]
-    f32 = jnp.float32
+    total = src.shape[1]
+    per_request = total // REQS
 
     def iota(cols, axis):
-        return lax.broadcasted_iota(jnp.int32, (per_dev, cols), axis).astype(f32)
-
-    def over(row, by):
-        return jnp.floor(row * (1.0 / by))
-
-    src, dst = src_ref[...].astype(f32), dst_ref[...].astype(f32)
-    lane, sub = iota(total, 1), iota(total, 0)
-    own = lane == sub + (me * per_dev).astype(f32)
+        return lax.broadcasted_iota(jnp.int32, (per_dev, cols), axis)
+
+    lane = iota(total, 1)
+    own = lane == iota(total, 0) + me * per_dev
     small_lane, small_sub = iota(per_dev, 1), iota(per_dev, 0)
 
     def column(mask, row):
-        return jnp.sum(jnp.where(mask, row, 0.0), axis=1, keepdims=True)
+        return jnp.sum(jnp.where(mask, row, 0), axis=1, keepdims=True)
 
     def as_row(col):
-        return jnp.sum(jnp.where(small_lane == small_sub, col, 0.0), axis=0, keepdims=True)
+        return jnp.sum(jnp.where(small_lane == small_sub, col, 0), axis=0, keepdims=True)
 
     src_ids = column(own, src)
-    dst_ids = column(own, dst)
     target = over(column(src_ids == dst, lane), per_dev)
     same = (target == as_row(target)) & (small_lane < small_sub)
-    bucket = target * cap + column(same, 1.0)
-    slots = iota(send_index.shape[1], 1)
-    filled = jnp.where(bucket == slots, iota(send_index.shape[1], 0), 0.0)
-    send_index[...] = jnp.sum(filled, axis=0, keepdims=True).astype(jnp.int32)
-
-    root = column(dst_ids == src, lane)
+    bucket = target * cap + column(same, 1)
+    slots = send_index.shape[1]
+    filled = jnp.where(bucket == iota(slots, 1), iota(slots, 0), 0)
+    send_index[...] = jnp.sum(filled, axis=0, keepdims=True)
+
+    root = column(column(own, dst) == src, lane)
     owner = over(root, per_dev)
     earlier = (owner == as_row(owner)) & (as_row(root) < root)
-    take_index[...] = as_row(owner * cap + column(earlier, 1.0)).astype(jnp.int32)
+    take_index[...] = as_row(owner * cap + column(earlier, 1))
 
     token, block = iota(per_dev * block_len, 1), iota(per_dev * block_len, 0)
     holds = over(token, block_len) == block
-    ids = jnp.sum(jnp.where(holds, src_ids, 0.0), axis=0, keepdims=True)
-    inner = token[:1] - over(token[:1], block_len) * block_len
+    ids = jnp.sum(jnp.where(holds, src_ids, 0), axis=0, keepdims=True)
     request = over(ids, per_request)
-    at = (ids - request * per_request) * block_len + inner
+    at = (ids - request * per_request) * block_len + (token[:1] & (block_len - 1))
     limit = jnp.zeros_like(at)
     for r in range(REQS):
-        limit = jnp.where(request == r, lengths[r].astype(f32), limit)
-    tokens_of[...] = jnp.where(at < limit, request, -1.0).astype(jnp.int32)
-
-
-def plan(n, per_dev, block_len, src_blocks, dst_blocks, lengths):
-    total = src_blocks.shape[0]
-    slots = -(-n * ((per_dev + n - 1) // n) // HD) * HD
-    vmem = pl.BlockSpec(memory_space=pltpu.VMEM)
-    return pl.pallas_call(
-        functools.partial(plan_kernel, n, per_dev, block_len, total // REQS),
-        out_shape=(
-            jax.ShapeDtypeStruct((1, slots), jnp.int32),
-            jax.ShapeDtypeStruct((1, per_dev), jnp.int32),
-            jax.ShapeDtypeStruct((1, per_dev * block_len), jnp.int32),
-        ),
-        in_specs=[vmem, vmem, pl.BlockSpec(memory_space=pltpu.SMEM)],
-        out_specs=(vmem, vmem, vmem),
-        name="plan",
-    )(src_blocks.reshape(1, total), dst_blocks.reshape(1, total), lengths)
-
-
-def place_kernel(index, arrived, attn, placed, result, sems, attn_sem):
+        limit = jnp.where(request == r, lengths[r], limit)
+    tokens_of[...] = jnp.where(at < limit, request, -1)
+
+
+def place_kernel(
+    index, arrived, attn, placed, result, held, held_attn, in_sems, out_sems, attn_sems
+):
     cap = arrived.shape[1]
 
-    def write(i):
+    def read(i):
         at = index[0, i]
         return pltpu.make_async_copy(
-            arrived.at[at // cap, lax.rem(at, cap)], placed.at[i], sems.at[i]
+            arrived.at[at // cap, lax.rem(at, cap)], held.at[i], in_sems.at[i]
         )
 
+    def write(i):
+        return pltpu.make_async_copy(held.at[i], placed.at[i], out_sems.at[i])
+
     def loop(body):
-        lax.fori_loop(0, placed.shape[0], lambda i, c: (body(i), c)[1], 0)
-
-    attn_out = pltpu.make_async_copy(attn, result, attn_sem.at[0])
-    loop(lambda i: write(i).start())
+        lax.fori_loop(0, held.shape[0], lambda i, c: (body(i), c)[1], 0)
+
+    attn_in = pltpu.make_async_copy(attn, held_attn, attn_sems.at[0])
+    attn_out = pltpu.make_async_copy(held_attn, result, attn_sems.at[1])
+    attn_in.start()
+    loop(lambda i: read(i).start())
+    attn_in.wait()
     attn_out.start()
+    loop(lambda i: (read(i).wait(), write(i).start()))
     loop(lambda i: write(i).wait())
     attn_out.wait()
 
@@ -108,21 +96,23 @@
     count = index.shape[1]
     shape = (count,) + arrived.shape[2:]
     dma = pltpu.SemaphoreType.DMA
-    hbm = pl.BlockSpec(memory_space=pl.ANY)
-    vmem = pl.BlockSpec(memory_space=pltpu.VMEM)
+    hbm = pl.BlockSpec(memory_space=pltpu.HBM)
     return pl.pallas_call(
         place_kernel,
         out_shape=(
             jax.ShapeDtypeStruct(shape, arrived.dtype),
             jax.ShapeDtypeStruct(attn.shape, attn.dtype),
         ),
-        in_specs=[pl.BlockSpec(memory_space=pltpu.SMEM), vmem, vmem],
+        in_specs=[pl.BlockSpec(memory_space=pltpu.SMEM), hbm, hbm],
         out_specs=(hbm, hbm),
         scratch_shapes=[
+            pltpu.VMEM(shape, arrived.dtype),
+            pltpu.VMEM(attn.shape, attn.dtype),
             dma((count,)),
-            dma((1,)),
+            dma((count,)),
+            dma((2,)),
         ],
-        compiler_params=pltpu.CompilerParams(vmem_limit_bytes=16 * 1024 * 1024),
+        compiler_params=pltpu.CompilerParams(vmem_limit_bytes=60 * 1024 * 1024),
         name="place",
     )(index, arrived, attn)
 
@@ -143,15 +133,28 @@
     n,
     groups,
     halves,
-    send_index,
-    cache,
-    queries,
-    fresh_keys,
-    fresh_values,
-    token_request,
+    lengths,
+    *refs,
+):
+    *sources, arrived, result, take_index = refs[:9]
+    cache, queries, fresh_keys, fresh_values, src_blocks, dst_blocks = loaded = refs[9:15]
+    kernel_body(n, groups, halves, lengths, sources, loaded, arrived, result, take_index, *refs[15:])
+
+
+def kernel_body(
+    n,
+    groups,
+    halves,
+    lengths,
+    sources,
+    loaded,
     arrived,
     result,
+    take_index,
     outgoing,
+    send_vector,
+    send_index,
+    token_request,
     fresh_rows,
     fresh_bias,
     acc,
@@ -165,6 +168,7 @@
     pair_recv,
     own_sem,
 ):
+    cache, queries, fresh_keys, fresh_values, src_blocks, dst_blocks = loaded
     me = lax.axis_index("ctx")
     blocks, layers, _, block_len, _ = cache.shape
     tokens = blocks * block_len
@@ -192,6 +196,13 @@
             device_id_type=MESH,
         )
 
+    loads = [
+        pltpu.make_async_copy(src, dst, own_sem.at[1 + i])
+        for i, (src, dst) in enumerate(zip(sources, loaded))
+    ]
+    for load in loads[::-1]:
+        load.start()
+
     barrier = pltpu.get_barrier_semaphore()
     loop(
         1,
@@ -200,7 +211,25 @@
             barrier, 1, device_id={"ctx": peer(k)}, device_id_type=MESH
         ),
     )
+    loads[4].wait()
+    loads[5].wait()
+    plan(
+        n,
+        me,
+        blocks,
+        block_len,
+        src_blocks[...],
+        dst_blocks[...],
+        lengths,
+        send_vector,
+        take_index,
+        token_request,
+    )
+    index_copy = pltpu.make_async_copy(send_vector, send_index, own_sem.at[7])
+    index_copy.start()
     pl.semaphore_wait(barrier, n - 1)
+    index_copy.wait()
+    loads[0].wait()
 
     def block_copy(k):
         return send(
@@ -236,6 +265,8 @@
     fill(me)
     own_copy = pltpu.make_async_copy(outgoing.at[me], arrived.at[me], own_sem.at[0])
     own_copy.start()
+    for load in loads[1:4]:
+        load.wait()
 
     steps = queries.shape[0]
     heads = rows // steps
@@ -404,7 +435,8 @@
     loop(1, n, lambda k: block_copy(k).wait())
 
 
-def exchange(n, cap, send_index, cache, queries, fresh_keys, fresh_values, token_request):
+def exchange(n, cap, lengths, *arrays):
+    cache, queries = arrays[:2]
     steps, layers, requests, _ = queries.shape
     share = requests * KVH * QPG // n
     groups = max(share // QPG, 1)
@@ -414,6 +446,8 @@
     fresh_pad = -(-steps * requests // 16) * 16
     stages = n.bit_length() - 1
     block = cache.shape[1:]
+    per_dev, block_len = cache.shape[0], cache.shape[3]
+    slots = -(-n * cap // HD) * HD
     piece = (groups, layers, rows, HD)
     note = (groups, STAT_ROWS, HD)
     vmem = pl.BlockSpec(memory_space=pltpu.VMEM)
@@ -426,11 +460,16 @@
         out_shape=(
             jax.ShapeDtypeStruct((n, cap) + block, cache.dtype),
             jax.ShapeDtypeStruct((steps, layers, share, HD), f32),
+            jax.ShapeDtypeStruct((1, per_dev), jnp.int32),
         ),
-        in_specs=[smem] + [vmem] * 5,
-        out_specs=(hbm, vmem),
-        scratch_shapes=[
+        in_specs=[smem] + [pl.BlockSpec(memory_space=pltpu.HBM)] * len(arrays),
+        out_specs=(hbm, vmem, vmem),
+        scratch_shapes=[pltpu.VMEM(array.shape, array.dtype) for array in arrays]
+        + [
             pltpu.VMEM((n, cap) + block, cache.dtype),
+            pltpu.VMEM((1, slots), jnp.int32),
+            pltpu.SMEM((1, slots), jnp.int32),
+            pltpu.VMEM((1, per_dev * block_len), jnp.int32),
             pltpu.VMEM((2, layers, fresh_pad, KVH * HD), cache.dtype),
             pltpu.VMEM((requests * halves * rows, fresh_pad), f32),
             pltpu.VMEM((n,) + piece, f32),
@@ -442,24 +481,21 @@
             dma((n,)),
             dma((2, stages)),
             dma((2, stages)),
-            dma((1,)),
+            dma((8,)),
         ],
         compiler_params=pltpu.CompilerParams(
-            collective_id=0, has_side_effects=True, vmem_limit_bytes=32 * 1024 * 1024
+            collective_id=0, has_side_effects=True, vmem_limit_bytes=60 * 1024 * 1024
         ),
         name="exchange",
-    )(send_index, cache, queries, fresh_keys, fresh_values, token_request)
+    )(lengths, *arrays)
 
 
 def local(src_cache, src_blocks, dst_blocks, ctx_lengths, queries, new_keys, new_values):
     n = lax.axis_size("ctx")
-    per_dev, _, _, block_len, _ = src_cache.shape
-    cap = (per_dev + n - 1) // n
-    send_index, take_index, token_request = plan(
-        n, per_dev, block_len, src_blocks, dst_blocks, ctx_lengths
-    )
-    arrived, attn = exchange(
-        n, cap, send_index, src_cache, queries, new_keys, new_values, token_request
+    cap = (src_cache.shape[0] + n - 1) // n
+    tables = [blocks.reshape(1, -1) for blocks in (src_blocks, dst_blocks)]
+    arrived, attn, take_index = exchange(
+        n, cap, ctx_lengths, src_cache, queries, new_keys, new_values, *tables
     )
     return place(arrived, attn, take_index)
 

time: 117 us -> 112 us (0.957)
  the two profiles are of different devices: /device:TPU:0 before, /device:TPU:9 now
where the time goes in v6:
time: 112 us; the launch traced here: 110 us
  Pallas kernels  109 us (97%)
    pallas_call x1, Pallas kernels, exchange(): pl.pallas_call(functools.partial(exchange_kernel, n, groups, halves), out...  104 us
    pallas_call x1, Pallas kernels, place(): pl.pallas_call(place_kernel, out_shape=(jax.ShapeDtypeStruct(shape, arriv...  5.42 us

profile of v6, /device:TPU:9, one launch (start us, length us, event | category | flops | bytes accessed | tf_op | source)
XLA Modules:
  0.0 110.1 jit_solution(18011283018453717976)
XLA Ops:
  0.6 104.0 %exchange.1 = (bf16[16,2,2,2,16,1024]{5,4,3,2,1,0:T(8,128)(2,1)}, f32[5,2,32,128]{3,2,1,0:T(8,128)}, s32[1,32]{1,0:T(1,128)}) custom-call(s32[4]{0:T(128)} %lengths.1, bf16[32,2,2,16,1024]{4,3,2,1,0:T(8,128)(2,1)} %refs_0_.1, bf16[5,2,4,16384]{3,2,1,0:T(4,128)(2,1)} %refs_1_.1, bf16[5,2,4,1024]{3,2,1,0:T(4,128)(2,1)} %refs_2_.1, ...), custom_call_target="tpu_custom_call" | custom-call | tf_op jit(solution)/shard_map/exchange/pallas_call | solution.py:458
  104.7 5.4 %place.1 = (bf16[32,2,2,16,1024]{4,3,2,1,0:T(8,128)(2,1)}, f32[5,2,32,128]{3,2,1,0:T(8,128)}) custom-call(s32[1,32]{1,0:T(1,128)} %get-tuple-element.5.index, bf16[16,2,2,2,16,1024]{5,4,3,2,1,0:T(8,128)(2,1)} %get-tuple-element.6.arrived, f32[5,2,32,128]{3,2,1,0:T(8,128)} %get-tuple-element.7.attn), custom_call_target="tpu_custom_call" | custom-call | tf_op jit(solution)/shard_map/place/pallas_call | solution.py:100

commit v7 on v6

--- a/solution.py
+++ b/solution.py
@@ -14,6 +14,8 @@
 
 NEG_BIG = -1e30
 STAT_ROWS = 8
+LEVELS = 32767.0
+TINY = 1e-30
 MESH = pl.DeviceIdType.MESH
 
 
@@ -78,17 +80,25 @@
     def write(i):
         return pltpu.make_async_copy(held.at[i], placed.at[i], out_sems.at[i])
 
-    def loop(body):
-        lax.fori_loop(0, held.shape[0], lambda i, c: (body(i), c)[1], 0)
+    count = held.shape[0]
+    window = min(8, count)
+
+    def loop(start, stop, body):
+        lax.fori_loop(start, stop, lambda i, c: (body(i), c)[1], 0)
 
     attn_in = pltpu.make_async_copy(attn, held_attn, attn_sems.at[0])
     attn_out = pltpu.make_async_copy(held_attn, result, attn_sems.at[1])
     attn_in.start()
-    loop(lambda i: read(i).start())
+    loop(0, window, lambda i: read(i).start())
     attn_in.wait()
     attn_out.start()
-    loop(lambda i: (read(i).wait(), write(i).start()))
-    loop(lambda i: write(i).wait())
+    loop(
+        0,
+        count - window,
+        lambda i: (read(i).wait(), write(i).start(), read(i + window).start()),
+    )
+    loop(count - window, count, lambda i: (read(i).wait(), write(i).start()))
+    loop(0, count, lambda i: write(i).wait())
     attn_out.wait()
 
 
@@ -159,6 +169,8 @@
     fresh_bias,
     acc,
     acc_in,
+    coded,
+    coded_in,
     stat,
     stat_in,
     stat_cols,
@@ -389,6 +401,26 @@
                     + acc_new[gi, layer] * factor[:rows, layers + layer : layers + layer + 1]
                 )
 
+    def encode(acc_own, stat_own):
+        for gi in range(groups):
+            scales = jnp.zeros((rows, HD), jnp.float32)
+            for layer in range(layers):
+                value = acc_own[gi, layer]
+                peak = jnp.max(jnp.abs(value), axis=1, keepdims=True)
+                scale = jnp.maximum(peak, TINY) * (1.0 / LEVELS)
+                steps_of = jnp.round(value / scale).astype(jnp.int32)
+                coded[0, gi, layer] = steps_of.astype(jnp.int16)
+                scales = jnp.where(lane == layer, scale, scales)
+            turned = jnp.concatenate([scales, pad], axis=0).T
+            stat_own[gi, 2 * layers : 3 * layers] = turned[:layers]
+
+    def decode(at):
+        for gi in range(groups):
+            factor = columns(stat_in[at, gi, 2 * layers : 3 * layers])
+            for layer in range(layers):
+                value = coded_in[0, gi, layer].astype(jnp.int32).astype(jnp.float32)
+                acc_in[at, gi, layer] = value * factor[:rows, layer : layer + 1]
+
     base = 0
     for stage in range(stages):
         half = n // 2 ** (stage + 1)
@@ -396,21 +428,22 @@
         partner = me + 2**stage * (1 - 2 * bit)
         keep, give = base + bit * half, base + (1 - bit) * half
         at = n - 2 * half
+        last = stage == stages - 1
+        if last:
+            encode(acc.at[give], stat.at[give])
+        sums = (coded, coded_in) if last else (acc.at[pl.ds(give, half)], acc_in.at[pl.ds(at, half)])
+        notes = (stat.at[pl.ds(give, half)], stat_in.at[pl.ds(at, half)])
         copies = [
-            send(
-                src.at[pl.ds(give, half)],
-                dst.at[pl.ds(at, half)],
-                pair_send.at[i, stage],
-                pair_recv.at[i, stage],
-                partner,
-            )
-            for i, (src, dst) in enumerate(((stat, stat_in), (acc, acc_in)))
+            send(src, dst, pair_send.at[i, stage], pair_recv.at[i, stage], partner)
+            for i, (src, dst) in enumerate((notes, sums))
         ]
         for copy in copies:
             copy.start()
         loop(windows[2 + stage], windows[3 + stage], send_blocks)
         for copy in copies:
             copy.wait()
+        if last:
+            decode(at)
         loop(
             0,
             half,
@@ -474,6 +507,8 @@
             pltpu.VMEM((requests * halves * rows, fresh_pad), f32),
             pltpu.VMEM((n,) + piece, f32),
             pltpu.VMEM((n - 1,) + piece, f32),
+            pltpu.VMEM((1,) + piece, jnp.int16),
+            pltpu.VMEM((1,) + piece, jnp.int16),
             pltpu.VMEM((n,) + note, f32),
             pltpu.VMEM((n - 1,) + note, f32),
             pltpu.VMEM((requests * halves * rows, HD), f32),

time: 112 us -> 112 us (level)
  the two profiles are of different devices: /device:TPU:9 before, /device:TPU:0 now
where the time goes in v7:
time: 112 us; the launch traced here: 111 us
  Pallas kernels  111 us (99%)
    pallas_call x1, Pallas kernels, exchange(): pl.pallas_call(functools.partial(exchange_kernel, n, groups, halves), out...  104 us
    pallas_call x1, Pallas kernels, place(): pl.pallas_call(place_kernel, out_shape=(jax.ShapeDtypeStruct(shape, arriv...  6.75 us

profile of v7, /device:TPU:0, one launch (start us, length us, event | category | flops | bytes accessed | tf_op | source)
XLA Modules:
  0.0 111.4 jit_solution(12069365549044836180)
XLA Ops:
  0.6 104.0 %exchange.1 = (bf16[16,2,2,2,16,1024]{5,4,3,2,1,0:T(8,128)(2,1)}, f32[5,2,32,128]{3,2,1,0:T(8,128)}, s32[1,32]{1,0:T(1,128)}) custom-call(s32[4]{0:T(128)} %lengths.1, bf16[32,2,2,16,1024]{4,3,2,1,0:T(8,128)(2,1)} %refs_0_.1, bf16[5,2,4,16384]{3,2,1,0:T(4,128)(2,1)} %refs_1_.1, bf16[5,2,4,1024]{3,2,1,0:T(4,128)(2,1)} %refs_2_.1, ...), custom_call_target="tpu_custom_call" | custom-call | tf_op jit(solution)/shard_map/exchange/pallas_call | solution.py:491
  104.7 6.7 %place.1 = (bf16[32,2,2,16,1024]{4,3,2,1,0:T(8,128)(2,1)}, f32[5,2,32,128]{3,2,1,0:T(8,128)}) custom-call(s32[1,32]{1,0:T(1,128)} %get-tuple-element.5.index, bf16[16,2,2,2,16,1024]{5,4,3,2,1,0:T(8,128)(2,1)} %get-tuple-element.6.arrived, f32[5,2,32,128]{3,2,1,0:T(8,128)} %get-tuple-element.7.attn), custom_call_target="tpu_custom_call" | custom-call | tf_op jit(solution)/shard_map/place/pallas_call | solution.py:110
